TPU v7x, 32 devices: a whole 2x2x4 slice. The times are simulated.
32 devices in a mesh: shard: 8 (over z, y), rep: 4 (over x, core).
Axes of the slice: x: 2, y: 2, z: 4, core: 2. Of those that a mesh axis runs over, the one named last changes fastest.
Arguments:
- feature_table: bfloat16 [2048, 1024], P('shard'), may hold values from -8 to 8
- projection: bfloat16 [1024, 1024], replicated, may hold values from -0.1875 to 0.1875
- slot_owner: int32 [1024, 16, 1], P(('shard', 'rep')), may hold values from 0 to 7; in each aligned block of 512 rows (0 to 511, 512 to 1023, ..., all dimensions but the last counted through in order) at most 128 rows name the same one
- slot_row: int32 [1024, 16], P(('shard', 'rep')), may hold values from 0 to 255
- visits: int32 [1024, 13], P(('shard', 'rep')), may hold values from 1 to 32
- neg_row: int32 [512], P('shard'), may hold values from 0 to 255
Outputs:
- table_grad: float32 [2048, 1024], P('shard')
Inputs may be any that keep to these rules, and one draw needn't show every extreme that they name: `slot_owner`: within the slots of one device's 32 queries (aligned blocks of 512 slots in order), no shard index is named more than 128 times, a bound that some block reaches. `neg_row`: negative j lies in the rows of shard index j // 64.
All inputs are finite; a program needn't handle non-finite values.
Results may differ from a plain program's by a relative error of at most 0.006.
Values may be sent and summed in bfloat16 or wider, within the bound.
A program may use at most 64 MiB of HBM per device.

v0:
```python
import jax
import jax.numpy as jnp
from jax import lax
from jax.sharding import PartitionSpec as P

score_scale = 8.0
margin_value = 0.1
epsilon = 1e-06


def unit_rows(values):
    norms = jnp.sqrt(jnp.sum(values * values, axis=-1, keepdims=True) + epsilon)
    return (values / norms, norms)


def unit_back(grads, unit, norms):
    return (grads - unit * jnp.sum(unit * grads, axis=-1, keepdims=True)) / norms


def silu_slope(preact):
    gate_value = jax.nn.sigmoid(preact)
    return gate_value * (1.0 + preact * (1.0 - gate_value))


def times_back(left, projection):
    return jnp.einsum("re,fe->rf", left, projection, preferred_element_type=jnp.float32)


def on_device(feature_table, projection, slot_owner, slot_row, visits, neg_row):
    shard_count = lax.axis_size("shard")
    query_count, slot_count = slot_row.shape
    row_count = query_count * slot_count
    capacity = 2 * row_count // shard_count
    feat_width = projection.shape[0]
    embed_width = projection.shape[1]
    owners = slot_owner.reshape(row_count)
    one_hot = (owners[:, None] == jnp.arange(shard_count, dtype=jnp.int32)[None, :]).astype(
        jnp.int32
    )
    earlier = jnp.cumsum(one_hot, axis=0) - one_hot
    slot_rank = jnp.sum(earlier * one_hot, axis=1)
    position = owners * capacity + slot_rank
    send_ids = (
        jnp.zeros((shard_count * capacity,), jnp.int32)
        .at[position]
        .set(slot_row.reshape(row_count))
    )
    send_ids = send_ids.reshape(shard_count, capacity)
    asked = lax.all_to_all(send_ids, "shard", split_axis=0, concat_axis=0, tiled=True)
    picked = feature_table[asked]
    fetched = lax.all_to_all(picked, "shard", split_axis=0, concat_axis=0, tiled=True)
    gathered = fetched.reshape(shard_count * capacity, feat_width)[position]
    neg_pre = jnp.dot(feature_table[neg_row], projection, preferred_element_type=jnp.float32)
    neg_unit, neg_norms = unit_rows(jax.nn.silu(neg_pre))
    neg_embed = lax.all_gather(neg_unit.astype(jnp.bfloat16), "shard", axis=0, tiled=True)
    visit_float = visits.astype(jnp.float32)
    coefs = visit_float / jnp.sum(visit_float, axis=1, keepdims=True)
    preact = jnp.dot(gathered, projection, preferred_element_type=jnp.float32).reshape(
        query_count, slot_count, embed_width
    )
    active = jax.nn.silu(preact)
    hood = active[:, 0] + jnp.einsum("bk,bke->be", coefs, active[:, 3:])
    query_unit, query_norms = unit_rows(hood)
    query_embed = query_unit.astype(jnp.bfloat16)
    item_unit, item_norms = unit_rows(active[:, 1:3])
    item_embed = item_unit.astype(jnp.bfloat16)
    query_float = query_embed.astype(jnp.float32)
    item_float = item_embed.astype(jnp.float32)
    neg_scores = jnp.einsum("be,ne->bn", query_embed, neg_embed, preferred_element_type=jnp.float32)
    pair_scores = jnp.sum(query_float[:, None, :] * item_float, axis=2)
    positive = pair_scores[:, 0:1]
    neg_weight = (
        score_scale * jax.nn.sigmoid(score_scale * (neg_scores - positive + margin_value))
    ).astype(jnp.bfloat16)
    hard_weight = (
        score_scale * jax.nn.sigmoid(score_scale * (pair_scores[:, 1:2] - positive + margin_value))
    ).astype(jnp.bfloat16)
    hard_float = hard_weight.astype(jnp.float32)
    total_weight = jnp.sum(neg_weight.astype(jnp.float32), axis=1, keepdims=True) + hard_float
    query_grad = (
        jnp.dot(neg_weight, neg_embed, preferred_element_type=jnp.float32)
        + hard_float * item_float[:, 1]
        - total_weight * item_float[:, 0]
    )
    item_grad = jnp.stack([-total_weight * query_float, hard_float * query_float], axis=1)
    neg_partial = jnp.einsum(
        "bn,be->ne", neg_weight, query_embed, preferred_element_type=jnp.float32
    )
    hood_grad = unit_back(query_grad, query_unit, query_norms)
    item_back = unit_back(item_grad, item_unit, item_norms)
    active_grad = jnp.concatenate(
        [hood_grad[:, None], item_back, coefs[:, :, None] * hood_grad[:, None]], axis=1
    )
    preact_grad = (
        (active_grad * silu_slope(preact)).astype(jnp.bfloat16).reshape(row_count, embed_width)
    )
    outgoing = (
        jnp.zeros((shard_count * capacity, embed_width), jnp.bfloat16).at[position].set(preact_grad)
    )
    incoming = lax.all_to_all(
        outgoing.reshape(shard_count, capacity, embed_width),
        "shard",
        split_axis=0,
        concat_axis=0,
        tiled=True,
    )
    contrib = times_back(incoming.reshape(shard_count * capacity, embed_width), projection)
    neg_sum = lax.psum_scatter(neg_partial, "shard", scatter_dimension=0, tiled=True)
    grad_local = (
        jnp.zeros((feature_table.shape[0], feat_width), jnp.float32)
        .at[asked.reshape(-1)]
        .add(contrib)
    )
    grad_local, neg_total = lax.psum((grad_local, neg_sum), "rep")
    neg_back = unit_back(neg_total, neg_unit, neg_norms)
    neg_pre_grad = (neg_back * silu_slope(neg_pre)).astype(jnp.bfloat16)
    neg_rows = times_back(neg_pre_grad, projection)
    return grad_local.at[neg_row].add(neg_rows)


def solution(mesh):
    return jax.shard_map(
        on_device,
        mesh=mesh,
        in_specs=(
            P("shard", None),
            P(),
            P(("shard", "rep"), None, None),
            P(("shard", "rep"), None),
            P(("shard", "rep"), None),
            P("shard"),
        ),
        out_specs=P("shard", None),
        check_vma=False,
    )
```

profile of v0, /device:TPU:1, one launch (start us, length us, event | category | flops | bytes accessed | tf_op | source)
XLA Modules:
  0.0 273.7 jit_solution(9913302412486486817)
XLA Ops:
  6.5 0.9 copy.13
  7.5 0.1 eq.29
  7.5 0.1 eq.25
  7.6 0.7 broadcast_multiply_fusion.1
  8.3 1.1 reduce-window.6
  9.5 0.2 slice_reduce_fusion
  9.7 0.1 copy.12
  9.8 0.1 mul.161
  9.9 0.8 copy.15
  10.7 0.1 reshape.187
  10.8 0.1 fusion.30
  10.9 2.4 scatter_custom_fusion
  13.3 11.5 %all_to_all.22 = s32[8,1,128]{2,1,0:T(1,128)S(1)} all-to-all(s32[8,1,128]{2,1,0:T(1,128)S(1)} %bitcast.102), channel_id=1, replica_groups=mesh['shard'=8,'rep'=4] {'shard'}, dimensions={0} | all-to-all | bytes 8192 | tf_op jit(solution)/shard_map/all_to_all | solution.py:49
  24.8 7.2 %gather_fusion = bf16[1024,1024]{1,0:T(8,128)(2,1)} fusion(bf16[256,1024]{1,0:T(8,128)(2,1)} %param.6, s32[1024]{0:T(1024)S(1)} %fusion.33), kind=kCustom, calls=%fused_computation | custom fusion | bytes 4198400 | tf_op jit(solution)/shard_map/gather | solution.py:50
  32.0 4.5 %all-to-all-start.1 = ((bf16[8,128,1024]{2,1,0:T(8,128)(2,1)}), bf16[8,128,1024]{2,1,0:T(8,128)(2,1)}, u32[]{:S(2)}, u32[]{:S(2)}) async-start(bf16[8,128,1024]{2,1,0:T(8,128)(2,1)} %bitcast.97), calls=%async_computation.1 | async-start | bytes 4194304 | tf_op jit(solution)/shard_map/all_to_all | solution.py:51
  36.5 0.2 all-gather.2.cloned.1.call-start
  36.7 0.0 copy-start.7
  36.8 0.7 gather_fusion.2
  37.5 0.6 multiply_reduce_fusion.3
  38.1 0.8 fusion.39
  38.9 0.0 all-gather.2.cloned.1.call-update
  38.9 0.0 copy-done.7
  38.9 0.1 copy.21
  39.0 0.1 copy.18
  39.1 51.0 %all-to-all-done.1 = bf16[8,128,1024]{2,1,0:T(8,128)(2,1)} async-done(((bf16[8,128,1024]{2,1,0:T(8,128)(2,1)}), bf16[8,128,1024]{2,1,0:T(8,128)(2,1)}, u32[]{:S(2)}, u32[]{:S(2)}) %all-to-all-start.1) | async-done | bytes 2097184 | tf_op jit(solution)/shard_map/all_to_all | solution.py:51
  90.2 4.6 %gather_fusion.1 = bf16[512,1024]{1,0:T(8,128)(2,1)S(1)} fusion(bf16[1024,1024]{1,0:T(8,128)(2,1)} %bitcast.10, s32[1024]{0:T(1024)S(1)} %pad_clamp_fusion.1), kind=kCustom, calls=%fused_computation.1 | custom fusion | bytes 2099200 | tf_op jit(solution)/shard_map/gather | solution.py:52
  94.8 1.2 fusion.41
  96.0 1.4 divide_multiply_fusion
  97.4 0.1 slice.44
  97.5 0.6 fusion.2
  98.1 0.1 multiply_reduce_fusion.6
  98.3 0.1 multiply_reduce_fusion.2
  98.4 0.1 fusion.40
  98.5 0.2 convert_convert_fusion
  98.7 0.0 copy-done.5
  98.7 0.0 all-gather.2.cloned.1.call-done
  98.7 1.8 convert_reduce_fusion
  100.6 0.1 multiply_bitcast_fusion.1
  100.7 1.3 fusion.6
  102.0 0.2 copy.20
  102.2 0.0 copy-done.6
  102.2 0.4 multiply_reduce_fusion.5
  102.6 0.1 subtract_divide_fusion
  102.7 0.2 broadcast_multiply_fusion
  102.9 0.1 copy.19
  103.1 0.6 pad_maximum_fusion
  103.6 1.0 copy-done.4
  104.6 0.8 fusion.1
  105.4 4.2 %scatter_custom_fusion.1 = bf16[1024,1024]{1,0:T(8,128)(2,1)} fusion(s32[512]{0:T(512)S(1)} %bitcast.105, bf16[512,1024]{1,0:T(8,128)(2,1)S(1)} %fusion.1, bf16[]{:T(256)} %constant.15.clone.1), kind=kCustom, calls=%fused_computation.29 | custom fusion | bytes 2097154 | tf_op jit(solution)/shard_map/scatter | solution.py:98
  109.6 10.2 %all-to-all-start.2 = ((bf16[8,128,1024]{2,1,0:T(8,128)(2,1)}), bf16[8,128,1024]{2,1,0:T(8,128)(2,1)}, u32[]{:S(2)}, u32[]{:S(2)}) async-start(bf16[8,128,1024]{2,1,0:T(8,128)(2,1)} %bitcast.99), calls=%async_computation.2 | async-start | bytes 4194304 | tf_op jit(solution)/shard_map/all_to_all | solution.py:100
  119.7 0.0 reduce-scatter.2.cloned.1.call-start
  119.8 1.8 fusion.43
  121.6 0.0 reduce-scatter.2.cloned.1.call-update
  121.6 0.3 all-reduce.3.cloned.1.call-start
  121.9 61.1 %all-to-all-done.2 = bf16[8,128,1024]{2,1,0:T(8,128)(2,1)} async-done(((bf16[8,128,1024]{2,1,0:T(8,128)(2,1)}), bf16[8,128,1024]{2,1,0:T(8,128)(2,1)}, u32[]{:S(2)}, u32[]{:S(2)}) %all-to-all-start.2) | async-done | bytes 2097184 | tf_op jit(solution)/shard_map/all_to_all | solution.py:100
  183.0 5.9 %fusion.42 = f32[1024,1024]{1,0:T(8,128)} fusion(bf16[1024,1024]{1,0:T(8,128)(2,1)} %bitcast.27, bf16[1024,1024]{1,0:T(8,128)(2,1)S(1)} %copy-done), kind=kOutput, calls=%fused_computation.97 | convolution fusion | flops 2147483648 | bytes 8388608 | tf_op jit(solution)/shard_map/re,fe->rf/dot_general | solution.py:26
  188.8 11.3 %scatter_custom_fusion.2 = f32[256,1024]{1,0:T(8,128)} fusion(s32[1024]{0:T(1024)S(1)} %bitcast.107, f32[1024,1024]{1,0:T(8,128)} %fusion.42, f32[]{:T(128)} %constant.10.clone.1), kind=kCustom, calls=%fused_computation.31 | custom fusion | flops 1048576 | bytes 1049088 | tf_op jit(solution)/shard_map/scatter-add | solution.py:112
  200.1 18.7 %reduce-scatter.2.cloned.1.call-done = f32[64,1024]{1,0:T(8,128)} async-done(((f32[512,1024]{1,0:T(8,128)}), f32[64,1024]{1,0:T(8,128)}) %reduce-scatter.2.cloned.1.call-update) | async-done | bytes 262160 | tf_op jit(solution)/shard_map/reduce_scatter | solution.py:108
  218.8 0.0 all-reduce.3.cloned.1.call-update
  218.8 41.8 %all-reduce.3.cloned.1.call-done = (f32[256,1024]{1,0:T(8,128)}, f32[64,1024]{1,0:T(8,128)}) async-done(((f32[256,1024]{1,0:T(8,128)}, f32[64,1024]{1,0:T(8,128)}), (f32[256,1024]{1,0:T(8,128)}, f32[64,1024]{1,0:T(8,128)})) %all-reduce.3.cloned.1.call-update) | async-done | bytes 1310736 | tf_op jit(solution)/shard_map/psum | solution.py:114
  260.6 1.2 multiply_reduce_fusion
  261.7 2.5 fusion.22
  264.3 1.9 scatter_fusion
  266.2 1.0 copy.36
  (32 shorter events, 0.2 us)
Async XLA Ops:
  6.5 30.9 %copy-start = (bf16[1024,1024]{1,0:T(8,128)(2,1)S(1)}, bf16[1024,1024]{1,0:T(8,128)(2,1)}, u32[]{:S(2)}) copy-start(bf16[1024,1024]{1,0:T(8,128)(2,1)} %param.7) | copy-start | bytes 6291460
  32.0 4.7 %copy-start.8 = (s32[64]{0:T(128)S(1)}, s32[64]{0:T(128)}, u32[]{:S(2)}) copy-start(s32[64]{0:T(128)} %param.11) | copy-start | bytes 772
  32.0 4.7 %copy-start.1 = (bf16[256,1024]{1,0:T(8,128)(2,1)S(1)}, bf16[256,1024]{1,0:T(8,128)(2,1)}, u32[]{:S(2)}) copy-start(bf16[256,1024]{1,0:T(8,128)(2,1)} %param.6) | copy-start | bytes 1572868
  32.0 58.2 %all-to-all-start.1 = ((bf16[8,128,1024]{2,1,0:T(8,128)(2,1)}), bf16[8,128,1024]{2,1,0:T(8,128)(2,1)}, u32[]{:S(2)}, u32[]{:S(2)}) async-start(bf16[8,128,1024]{2,1,0:T(8,128)(2,1)} %bitcast.97), calls=%async_computation.1 | async-start | bytes 4194304 | tf_op jit(solution)/shard_map/all_to_all | solution.py:51
  36.5 62.2 %all-gather.2.cloned.1.call-start = ((), (), s32[]{:S(2)}) async-start(), calls=%async_computation.4 | async-start | bytes 1179648 | tf_op jit(solution)/shard_map/all_gather | solution.py:55
  36.7 2.1 copy-start.7
  96.0 1.4 copy-start.3
  97.4 1.3 copy-start.5
  100.6 1.6 copy-start.6
  103.1 1.6 copy-start.4
  109.6 73.4 %all-to-all-start.2 = ((bf16[8,128,1024]{2,1,0:T(8,128)(2,1)}), bf16[8,128,1024]{2,1,0:T(8,128)(2,1)}, u32[]{:S(2)}, u32[]{:S(2)}) async-start(bf16[8,128,1024]{2,1,0:T(8,128)(2,1)} %bitcast.99), calls=%async_computation.2 | async-start | bytes 4194304 | tf_op jit(solution)/shard_map/all_to_all | solution.py:100
  119.7 99.1 %reduce-scatter.2.cloned.1.call-start = ((), (), s32[]{:S(2)}) async-start(), calls=%async_computation.5 | async-start | bytes 2359296 | tf_op jit(solution)/shard_map/reduce_scatter | solution.py:108
  121.6 139.0 %all-reduce.3.cloned.1.call-start = ((), (), s32[]{:S(2)}) async-start(), calls=%async_computation.6 | async-start | bytes 2621440 | tf_op jit(solution)/shard_map/psum | solution.py:114
  261.7 2.5 copy-start.2
Sparse Core Ops, SparseCore 0:
  39.4 58.0 all-gather.1
  124.1 94.6 reduce-scatter.1
  221.3 39.2 all-reduce.2
where the time goes:
time: 275 us; the launch traced here: 274 us
  waiting for transfers between devices  173 us (63%)
  local copies, waits for them, and re-layouts  24.1 us (9%)
  other arithmetic  22.1 us (8%)
  starting transfers between devices  15.2 us (6%)
  matrix products  14.8 us (5%)
  between operations  13.4 us (5%)
  blocking collectives  11.5 us (4%)
    all_to_all x1, waiting for transfers between devices, on_device(): lax.all_to_all(outgoing.reshape(shard_count, capacity, embed_width), 'sha...  61.1 us
    all_to_all x1, waiting for transfers between devices, on_device(): lax.all_to_all(picked, 'shard', split_axis=0, concat_axis=0, tiled=True)  51 us
    psum x1, waiting for transfers between devices, on_device(): grad_local, neg_total = lax.psum((grad_local, neg_sum), 'rep')  41.8 us
    reduce_scatter x1, waiting for transfers between devices, on_device(): lax.psum_scatter(neg_partial, 'shard', scatter_dimension=0, tiled=True)  18.7 us
    all_to_all x1, blocking collectives, on_device(): lax.all_to_all(send_ids, 'shard', split_axis=0, concat_axis=0, tiled=True)  11.5 us
    scatter-add x1, other arithmetic, on_device(): grad_local = jnp.zeros((feature_table.shape[0], feat_width), jnp.float32)...  11.3 us
    all_to_all x1, starting transfers between devices, on_device(): lax.all_to_all(outgoing.reshape(shard_count, capacity, embed_width), 'sha...  10.2 us
    dot_general x2, matrix products, times_back(): jnp.einsum('re,fe->rf', left, projection, preferred_element_type=jnp.floa...  8.41 us
  transfers between devices with their start and end apart: 5, of which 4 were waited for; matrix products, arithmetic and copies ran while one was open for 11% of the time, Pallas kernels for 0%

commit v1 on v0

--- a/solution.py
+++ b/solution.py
@@ -118,9 +118,140 @@
     return grad_local.at[neg_row].add(neg_rows)
 
 
+def row_picks(info, slot_count, node_count):
+    rows = info.shape[0]
+    ids = info[:, :slot_count]
+    visits = info[:, slot_count:]
+    lane = lax.broadcasted_iota(jnp.int32, (rows, node_count), 1)
+    singles = [(ids[:, s : s + 1] == lane).astype(jnp.bfloat16) for s in range(3)]
+    spread = jnp.zeros((rows, node_count), jnp.float32)
+    for k in range(slot_count - 3):
+        count = visits[:, k : k + 1].astype(jnp.float32)
+        spread = spread + jnp.where(ids[:, 3 + k : 4 + k] == lane, count, 0.0)
+    return jnp.concatenate(singles + [spread.astype(jnp.bfloat16)], axis=0)
+
+
+def column_split(feature_table, projection, slot_owner, slot_row, visits, neg_row):
+    shard_count = lax.axis_size("shard")
+    rep_count = lax.axis_size("rep")
+    query_count, slot_count = slot_row.shape
+    node_count = feature_table.shape[0]
+    neg_count = neg_row.shape[0]
+    embed_width = projection.shape[1]
+    width = embed_width // shard_count
+    group = query_count * shard_count
+    held = node_count + neg_count
+    f32, bf16 = jnp.float32, jnp.bfloat16
+    node = slot_owner[:, :, 0] * node_count + slot_row
+    info = lax.all_gather(jnp.concatenate([node, visits], axis=1), "shard", axis=0, tiled=True)
+    neg_pick = (neg_row[:, None] == jnp.arange(node_count, dtype=jnp.int32)[None, :]).astype(bf16)
+    neg_feat = jnp.dot(neg_pick, feature_table, preferred_element_type=f32).astype(bf16)
+    pre = jnp.dot(
+        jnp.concatenate([feature_table, neg_feat], axis=0), projection, preferred_element_type=f32
+    )
+    act = jax.nn.silu(pre)
+    neg_unit, neg_norms = unit_rows(act[node_count:])
+    rows = jnp.concatenate([act[:node_count], neg_unit], axis=0).astype(bf16)
+    slices = lax.all_to_all(
+        rows.reshape(held, shard_count, width).transpose(1, 0, 2), "shard", 0, 0, tiled=True
+    )
+    act_slice = slices[:, :node_count].reshape(shard_count * node_count, width)
+    neg_slice = slices[:, node_count:].reshape(shard_count * neg_count, width)
+    picks = row_picks(info, slot_count, shard_count * node_count)
+    picked = jnp.dot(picks, act_slice, preferred_element_type=f32)
+    total = jnp.sum(info[:, slot_count:].astype(f32), axis=1, keepdims=True)
+    own, pos, hard, spread = [picked[i * group : (i + 1) * group] for i in range(4)]
+    hood = own + spread / total
+    partial = lax.dot_general(
+        hood.astype(bf16), neg_slice, (((1,), (1,)), ((), ())), preferred_element_type=f32
+    )
+    stats = jnp.stack(
+        [jnp.sum(a * b, axis=1) for a, b in ((hood, hood), (pos, pos), (hard, hard), (hood, pos), (hood, hard))],
+        axis=1,
+    )
+    parts = lax.all_to_all(
+        partial.astype(bf16).reshape(shard_count, query_count, -1), "shard", 0, 0, tiled=True
+    )
+    stats = lax.all_to_all(
+        stats.reshape(shard_count, query_count, -1), "shard", 0, 0, tiled=True
+    )
+    weight, scalars = loss_weights(
+        jnp.sum(parts.astype(f32), axis=0), jnp.sum(stats, axis=0)
+    )
+    weight = lax.all_gather(weight, "shard", axis=0, tiled=True)
+    scalars = lax.all_gather(scalars, "shard", axis=0, tiled=True)
+    grads, query_embed = query_side(hood, pos, hard, total, weight, scalars, neg_slice)
+    node_part = lax.dot_general(
+        picks, grads, (((0,), (0,)), ((), ())), preferred_element_type=f32
+    )
+    neg_part = lax.dot_general(
+        weight, query_embed, (((0,), (0,)), ((), ())), preferred_element_type=f32
+    )
+    back = jnp.concatenate(
+        [
+            node_part.astype(bf16).reshape(shard_count, node_count, width),
+            neg_part.astype(bf16).reshape(shard_count, neg_count, width),
+        ],
+        axis=1,
+    )
+    back = lax.all_to_all(back, "shard", 0, 0, tiled=True)
+    back = back.transpose(1, 0, 2).reshape(rep_count, held // rep_count, embed_width)
+    back = jnp.sum(lax.all_to_all(back, "rep", 0, 0, tiled=True).astype(f32), axis=0)
+    back = lax.all_gather(back.astype(bf16), "rep", axis=0, tiled=True).astype(f32)
+    neg_grad = unit_back(back[node_count:], neg_unit, neg_norms)
+    neg_grad = (neg_grad * silu_slope(pre[node_count:])).astype(bf16)
+    pre_grad = back[:node_count] * silu_slope(pre[:node_count])
+    pre_grad = pre_grad + lax.dot_general(
+        neg_pick, neg_grad, (((0,), (0,)), ((), ())), preferred_element_type=f32
+    )
+    return times_back(pre_grad.astype(bf16), projection)
+
+
+def loss_weights(dots, stats):
+    inverse = lax.rsqrt(stats[:, 0:3] + epsilon)
+    scores = dots * inverse[:, 0:1]
+    positive = stats[:, 3:4] * inverse[:, 0:1] * inverse[:, 1:2]
+    hard = stats[:, 4:5] * inverse[:, 0:1] * inverse[:, 2:3]
+    weight = score_scale * jax.nn.sigmoid(score_scale * (scores - positive + margin_value))
+    weight = weight.astype(jnp.bfloat16)
+    wide = weight.astype(jnp.float32)
+    hard_weight = score_scale * jax.nn.sigmoid(score_scale * (hard - positive + margin_value))
+    hard_weight = hard_weight.astype(jnp.bfloat16).astype(jnp.float32)
+    total = jnp.sum(wide, axis=1, keepdims=True) + hard_weight
+    along = jnp.sum(wide * scores, axis=1, keepdims=True) + hard_weight * hard - total * positive
+    columns = [inverse, hard_weight, total, along, positive, hard]
+    return weight, jnp.concatenate(columns, axis=1)
+
+
+def query_side(hood, pos, hard, visit_total, weight, scalars, neg_slice):
+    f32, bf16 = jnp.float32, jnp.bfloat16
+    inv_q, inv_p, inv_h, hard_weight, total, along, pos_score, hard_score = [
+        scalars[:, i : i + 1] for i in range(8)
+    ]
+    query_unit, pos_unit, hard_unit = hood * inv_q, pos * inv_p, hard * inv_h
+    query_embed = query_unit.astype(bf16)
+    query_float = query_embed.astype(f32)
+    query_grad = (
+        jnp.dot(weight, neg_slice, preferred_element_type=f32)
+        + hard_weight * hard_unit.astype(bf16).astype(f32)
+        - total * pos_unit.astype(bf16).astype(f32)
+    )
+    hood_grad = (query_grad - query_unit * along) * inv_q
+    pos_grad = -total * (query_float - pos_unit * pos_score) * inv_p
+    hard_grad = hard_weight * (query_float - hard_unit * hard_score) * inv_h
+    grads = jnp.concatenate([hood_grad, pos_grad, hard_grad, hood_grad / visit_total], axis=0)
+    return grads.astype(bf16), query_embed
+
+
 def solution(mesh):
+    def body(feature_table, projection, *rest):
+        slice_width = projection.shape[1] // mesh.shape["shard"]
+        whole = slice_width >= 128 and slice_width % 128 == 0
+        form = column_split if whole else on_device
+        return form(feature_table, projection, *rest)
+
     return jax.shard_map(
-        on_device,
+        body,
         mesh=mesh,
         in_specs=(
             P("shard", None),

time: 275 us -> 196 us (0.71)
  waiting for transfers between devices: 173 us -> 10.1 us
  blocking collectives: 11.5 us -> 139 us
  local copies, waits for them, and re-layouts: 24.1 us -> 5.18 us
  between operations: 13.4 us -> 0.25 us
  other arithmetic: 22.1 us -> 12.4 us
    all_to_all x2 -> x3, waiting for transfers between devices: 112 us -> 10.1 us  [the longest x1 5.73 us: column_split(): lax.all_to_all(partial.astype(bf16).reshape(shard_count, query_count, -1)...]
    all_gather x0 -> x4, blocking collectives: none -> 90.1 us  [the longest x1 32.9 us: column_split(): lax.all_gather(jnp.concatenate([node, visits], axis=1), 'shard', axis=0,...]
    psum x1 -> x0, waiting for transfers between devices: 41.8 us -> none  [on_device(): grad_local, neg_total = lax.psum((grad_local, neg_sum), 'rep')]
    all_to_all x1 -> x2, blocking collectives: 11.5 us -> 48.6 us  [the longest x1 35 us: column_split(): lax.all_to_all(back, 'rep', 0, 0, tiled=True).astype(f32)]
    reduce_scatter x1 -> x0, waiting for transfers between devices: 18.7 us -> none  [on_device(): lax.psum_scatter(neg_partial, 'shard', scatter_dimension=0, tiled=True)]
    scatter-add x2 -> x0, other arithmetic: 13.2 us -> none  [the longest x1 11.3 us: on_device(): grad_local = jnp.zeros((feature_table.shape[0], feat_width), jnp.float32)...]
    gather x3 -> x0, local copies, waits for them, and re-layouts: 12.5 us -> none  [the longest x1 7.17 us: on_device(): picked = feature_table[asked]]
    convert_element_type x5, other arithmetic: 1.81 us -> 8.67 us  [the longest x1 4.55 us: row_picks(): return jnp.concatenate(singles + [spread.astype(jnp.bfloat16)], axis=0)]
  transfers between devices with their start and end apart: 5 -> 3, of which waited for: 4 -> 2; matrix products, arithmetic and copies ran while one was open for 11% -> 6% of each run, Pallas kernels for 0% -> 0%
where the time goes in v1:
time: 196 us; the launch traced here: 195 us
  blocking collectives  139 us (71%)
  matrix products  15.5 us (8%)
  starting transfers between devices  13.1 us (7%)
  other arithmetic  12.4 us (6%)
  waiting for transfers between devices  10.1 us (5%)
  local copies, waits for them, and re-layouts  5.18 us (3%)
    all_to_all x1, blocking collectives, column_split(): lax.all_to_all(back, 'rep', 0, 0, tiled=True).astype(f32)  35 us
    all_gather x1, blocking collectives, column_split(): lax.all_gather(jnp.concatenate([node, visits], axis=1), 'shard', axis=0,...  32.9 us
    all_gather x1, blocking collectives, column_split(): weight = lax.all_gather(weight, 'shard', axis=0, tiled=True)  25.1 us
    all_gather x1, blocking collectives, column_split(): scalars = lax.all_gather(scalars, 'shard', axis=0, tiled=True)  24 us
    all_to_all x1, blocking collectives, column_split(): back = lax.all_to_all(back, 'shard', 0, 0, tiled=True)  13.7 us
    all_gather x1, blocking collectives, column_split(): lax.all_gather(back.astype(bf16), 'rep', axis=0, tiled=True).astype(f32)  8.01 us
    all_to_all x1, starting transfers between devices, column_split(): lax.all_to_all(rows.reshape(held, shard_count, width).transpose(1, 0, 2),...  6.38 us
    all_to_all x1, waiting for transfers between devices, column_split(): lax.all_to_all(partial.astype(bf16).reshape(shard_count, query_count, -1)...  5.73 us
  transfers between devices with their start and end apart: 3, of which 2 were waited for; matrix products, arithmetic and copies ran while one was open for 6% of the time, Pallas kernels for 0%

profile of v1, /device:TPU:1, one launch (start us, length us, event | category | flops | bytes accessed | tf_op | source)
XLA Modules:
  0.0 195.2 jit_solution(8164474358767814821)
XLA Ops:
  0.0 0.0 copy-start
  0.0 1.4 convolution_convert_fusion.2
  1.5 0.3 copy-done
  1.8 3.0 %divide_multiply_fusion = (f32[320,1024]{1,0:T(8,128)S(1)}, f32[320,1024]{1,0:T(8,128)}) fusion(bf16[1024,1024]{1,0:T(8,128)(2,1)S(1)} %copy-done, bf16[64,1024]{1,0:T(8,128)(2,1)S(1)} %convolution_convert_fusion.2, bf16[256,1024]{1,0:T(8,128)(2,1)} %param.6), kind=kOutput, calls=%fused_computation.23 | convolution fusion | flops 673710080 | bytes 5373952 | tf_op jit(solution)/shard_map/dot_general | solution.py:149
  4.7 0.0 copy-start.1
  4.7 0.1 multiply_reduce_fusion.1
  4.9 0.0 copy-start.4
  4.9 0.0 copy-start.5
  4.9 0.0 copy-start.6
  4.9 0.1 copy_bitcast_fusion
  5.0 0.8 copy-done.1
  5.8 0.1 copy_bitcast_fusion.1
  5.9 0.9 maximum_bitcast_fusion
  6.8 6.4 %all-to-all-start = ((bf16[8,320,128]{2,1,0:T(8,128)(2,1)}), bf16[8,320,128]{2,1,0:T(8,128)(2,1)S(1)}, u32[]{:S(2)}, u32[]{:S(2)}) async-start(bf16[8,320,128]{2,1,0:T(8,128)(2,1)} %maximum_bitcast_fusion), calls=%async_computation | async-start | bytes 1310720 | tf_op jit(solution)/shard_map/all_to_all | solution.py:155
  13.2 0.0 copy-done.4
  13.2 0.1 copy.34
  13.3 0.0 copy-done.5
  13.3 0.1 copy.35
  13.3 0.0 copy-done.6
  13.3 0.1 copy.36
  13.4 0.1 pad_add_fusion
  13.5 32.9 %all_gather.12 = s32[256,29]{1,0:T(8,128)S(1)} all-gather(s32[32,29]{1,0:T(8,128)S(1)} %pad_add_fusion), channel_id=1, replica_groups=mesh['shard'=8,'rep'=4] {'shard'}, dimensions={0}, use_global_device_ids=true | all-gather | bytes 33408 | tf_op jit(solution)/shard_map/all_gather | solution.py:146
  46.4 0.2 fusion.37
  46.6 1.0 fusion.51
  47.6 1.2 slice_reduce_fusion.15
  48.8 1.8 fusion
  50.5 1.2 fusion.2
  51.8 4.5 %add_convert_fusion = bf16[256,2048]{1,0:T(8,128)(2,1)} fusion(f32[256]{0:T(256)S(1)} %get-tuple-element.27, s32[256]{0:T(256)S(1)} %get-tuple-element.11, f32[256]{0:T(256)S(1)} %get-tuple-element.28, s32[256]{0:T(256)S(1)} %get-tuple-element.12, f32[256]{0:T(256)S(1)} %get-tuple-element.29, s32[256]{0:T(256)S(1)} %get-tuple-element.13, ...), kind=kLoop, calls=%fused_computation.2 | loop fusion | flops 20447232 | bytes 1075200 | tf_op jit(solution)/shard_map/convert_element_type | solution.py:131
  56.3 0.0 all-to-all-done
  56.4 3.2 %fusion.17 = f32[1024,128]{0,1:T(8,128)S(1)} fusion(bf16[2048,128]{1,0:T(8,128)(2,1)S(1)} %bitcast.59, bf16[256,2048]{1,0:T(8,128)(2,1)} %add_convert_fusion, bf16[256,2048]{1,0:T(8,128)(2,1)} %fusion.2, bf16[256,2048]{1,0:T(8,128)(2,1)} %get-tuple-element.65, bf16[256,2048]{1,0:T(8,128)(2,1)} %get-tuple-element.64), kind=kOutput, calls=%fused_computation.44 | convolution fusion | flops 553648128 | bytes 5242880 | tf_op jit(solution)/shard_map/dot_general | solution.py:161
  59.6 0.1 multiply_reduce_fusion.2
  59.7 0.1 stack.22
  59.8 0.1 stack.21
  59.8 0.1 stack.19
  59.9 0.1 stack.20
  60.0 0.1 stack.18
  60.1 0.7 reshape.82
  60.8 3.3 %all-to-all-start.2 = ((f32[8,1,160]{2,1,0:T(1,128)}), f32[8,1,160]{2,1,0:T(1,128)S(1)}, u32[]{:S(2)}, u32[]{:S(2)}) async-start(f32[8,1,160]{2,1,0:T(1,128)} %reshape.82), calls=%async_computation.2 | async-start | bytes 16384 | tf_op jit(solution)/shard_map/all_to_all | solution.py:175
  64.1 1.0 convolution_convert_fusion.1
  65.1 4.3 %all-to-all-done.2 = f32[8,1,160]{2,1,0:T(1,128)S(1)} async-done(((f32[8,1,160]{2,1,0:T(1,128)}), f32[8,1,160]{2,1,0:T(1,128)S(1)}, u32[]{:S(2)}, u32[]{:S(2)}) %all-to-all-start.2) | async-done | bytes 5152 | tf_op jit(solution)/shard_map/all_to_all | solution.py:175
  69.4 3.4 %all-to-all-start.1 = ((bf16[8,32,512]{2,1,0:T(8,128)(2,1)}), bf16[8,32,512]{2,1,0:T(8,128)(2,1)S(1)}, u32[]{:S(2)}, u32[]{:S(2)}) async-start(bf16[8,32,512]{2,1,0:T(8,128)(2,1)} %bitcast.4), calls=%async_computation.1 | async-start | bytes 524288 | tf_op jit(solution)/shard_map/all_to_all | solution.py:172
  72.8 0.5 broadcast.82
  73.3 0.6 reduce.59
  74.0 0.1 reshape.83
  74.1 5.7 %all-to-all-done.1 = bf16[8,32,512]{2,1,0:T(8,128)(2,1)S(1)} async-done(((bf16[8,32,512]{2,1,0:T(8,128)(2,1)}), bf16[8,32,512]{2,1,0:T(8,128)(2,1)S(1)}, u32[]{:S(2)}, u32[]{:S(2)}) %all-to-all-start.1) | async-done | bytes 262176 | tf_op jit(solution)/shard_map/all_to_all | solution.py:172
  79.8 0.2 fusion.58
  80.1 24.0 %all-gather = f32[8,32,8]{1,2,0:T(8,128)S(1)} all-gather(f32[1,32,8]{1,2,0:T(8,128)S(1)} %bitcast.63), channel_id=1, replica_groups=mesh['shard'=8,'rep'=4] {'shard'}, dimensions={0}, use_global_device_ids=true | all-gather | bytes 9216 | tf_op jit(solution)/shard_map/all_gather | solution.py:182
  104.2 0.1 reshape.52
  104.3 25.1 %all_gather.13 = bf16[256,512]{1,0:T(8,128)(2,1)S(1)} all-gather(bf16[32,512]{1,0:T(8,128)(2,1)S(1)} %get-tuple-element.47), channel_id=1, replica_groups=mesh['shard'=8,'rep'=4] {'shard'}, dimensions={0}, use_global_device_ids=true | all-gather | bytes 294912 | tf_op jit(solution)/shard_map/all_gather | solution.py:181
  129.4 0.3 convolution_convert_fusion.3
  129.7 0.2 fusion.70
  130.0 0.0 copy-done.2
  130.0 0.0 copy-done.3
  130.0 2.9 %convolution_convert_fusion = bf16[2048,128]{1,0:T(8,128)(2,1)S(1)} fusion(bf16[256,2048]{1,0:T(8,128)(2,1)} %add_convert_fusion, bf16[256,2048]{1,0:T(8,128)(2,1)} %fusion.2, bf16[256,2048]{1,0:T(8,128)(2,1)S(1)} %copy-done.3, bf16[256,2048]{1,0:T(8,128)(2,1)S(1)} %copy-done.2, bf16[256,128]{0,1:T(8,128)(2,1)S(1)} %get-tuple-element.50, ...), kind=kOutput, calls=%fused_computation.1 | convolution fusion | flops 554958848 | bytes 4980736 | tf_op jit(solution)/shard_map/dot_general | solution.py:184
  132.9 13.7 %all_to_all.25 = bf16[8,320,128]{2,1,0:T(8,128)(2,1)S(1)} all-to-all(bf16[8,320,128]{2,1,0:T(8,128)(2,1)S(1)} %pad_maximum_fusion.3), channel_id=1, replica_groups=mesh['shard'=8,'rep'=4] {'shard'}, dimensions={0} | all-to-all | bytes 1310720 | tf_op jit(solution)/shard_map/all_to_all | solution.py:197
  146.6 0.4 copy.42
  147.0 0.3 reshape.50
  147.3 35.0 %all_to_all.26 = bf16[4,80,1024]{2,1,0:T(8,128)(2,1)S(1)} all-to-all(bf16[4,80,1024]{2,1,0:T(8,128)(2,1)S(1)} %reshape.50), channel_id=1, replica_groups=mesh['shard'=8,'rep'=4] {'rep'}, dimensions={0} | all-to-all | bytes 1310720 | tf_op jit(solution)/shard_map/all_to_all | solution.py:199
  182.3 0.1 reduce_sum.131
  182.4 8.0 %all_gather.15 = bf16[320,1024]{1,0:T(8,128)(2,1)S(1)} all-gather(bf16[80,1024]{1,0:T(8,128)(2,1)S(1)} %reduce_sum.131), channel_id=1, replica_groups=mesh['shard'=8,'rep'=4] {'rep'}, dimensions={0}, use_global_device_ids=true | all-gather | bytes 819200 | tf_op jit(solution)/shard_map/all_gather | solution.py:200
  190.4 0.1 convert_element_type.151
  190.5 1.2 multiply_reduce_fusion
  191.7 0.0 copy-done.7
  191.7 3.5 %fusion.4 = f32[256,1024]{1,0:T(8,128)} fusion(bf16[1024,1024]{1,0:T(8,128)(2,1)S(1)} %copy-done, f32[320,1024]{1,0:T(8,128)S(1)} %convert_element_type.151, f32[320,1024]{1,0:T(8,128)} %get-tuple-element.63, f32[64]{0:T(128)S(1)} %multiply_reduce_fusion, f32[64]{0:T(128)S(1)} %add_sqrt_fusion, s32[64]{0:T(128)S(1)} %copy-done.7, f32[320,1024]{1,0:T(8,128)} %copy-done.1), kind=kOutput, calls=%fused_computation.25 | convolution fusion | flops 573915136 | bytes 6030080 | tf_op jit(solution)/shard_map/re,fe->rf/dot_general | solution.py:26
  (24 shorter events, 0.3 us)
Async XLA Ops:
  0.0 1.8 copy-start
  4.7 1.1 copy-start.1
  4.9 8.3 %copy-start.4 = (s32[32,16,1]{0,2,1:T(1,128)S(1)}, s32[32,16,1]{0,2,1:T(1,128)}, u32[]{:S(2)}) copy-start(s32[32,16,1]{0,2,1:T(1,128)} %param.8) | copy-start | bytes 6148
  4.9 8.4 %copy-start.5 = (s32[32,16]{0,1:T(8,128)S(1)}, s32[32,16]{0,1:T(8,128)}, u32[]{:S(2)}) copy-start(s32[32,16]{0,1:T(8,128)} %param.9) | copy-start | bytes 6148
  4.9 8.5 %copy-start.6 = (s32[32,13]{0,1:T(8,128)S(1)}, s32[32,13]{0,1:T(8,128)}, u32[]{:S(2)}) copy-start(s32[32,13]{0,1:T(8,128)} %param.10) | copy-start | bytes 4996
  6.8 49.5 %all-to-all-start = ((bf16[8,320,128]{2,1,0:T(8,128)(2,1)}), bf16[8,320,128]{2,1,0:T(8,128)(2,1)S(1)}, u32[]{:S(2)}, u32[]{:S(2)}) async-start(bf16[8,320,128]{2,1,0:T(8,128)(2,1)} %maximum_bitcast_fusion), calls=%async_computation | async-start | bytes 1310720 | tf_op jit(solution)/shard_map/all_to_all | solution.py:155
  60.8 8.6 %all-to-all-start.2 = ((f32[8,1,160]{2,1,0:T(1,128)}), f32[8,1,160]{2,1,0:T(1,128)S(1)}, u32[]{:S(2)}, u32[]{:S(2)}) async-start(f32[8,1,160]{2,1,0:T(1,128)} %reshape.82), calls=%async_computation.2 | async-start | bytes 16384 | tf_op jit(solution)/shard_map/all_to_all | solution.py:175
  69.4 10.4 %all-to-all-start.1 = ((bf16[8,32,512]{2,1,0:T(8,128)(2,1)}), bf16[8,32,512]{2,1,0:T(8,128)(2,1)S(1)}, u32[]{:S(2)}, u32[]{:S(2)}) async-start(bf16[8,32,512]{2,1,0:T(8,128)(2,1)} %bitcast.4), calls=%async_computation.1 | async-start | bytes 524288 | tf_op jit(solution)/shard_map/all_to_all | solution.py:172
  104.2 25.7 %copy-start.2 = (bf16[256,2048]{1,0:T(8,128)(2,1)S(1)}, bf16[256,2048]{1,0:T(8,128)(2,1)}, u32[]{:S(2)}) copy-start(bf16[256,2048]{1,0:T(8,128)(2,1)} %get-tuple-element.64) | copy-start | bytes 3145732
  104.2 25.7 %copy-start.3 = (bf16[256,2048]{1,0:T(8,128)(2,1)S(1)}, bf16[256,2048]{1,0:T(8,128)(2,1)}, u32[]{:S(2)}) copy-start(bf16[256,2048]{1,0:T(8,128)(2,1)} %get-tuple-element.65) | copy-start | bytes 3145732
  182.3 9.4 %copy-start.7 = (s32[64]{0:T(128)S(1)}, s32[64]{0:T(128)}, u32[]{:S(2)}) copy-start(s32[64]{0:T(128)} %param.11) | copy-start | bytes 772

commit v2 on v0

--- a/solution.py
+++ b/solution.py
@@ -1,7 +1,13 @@
+import functools
+
 import jax
 import jax.numpy as jnp
 from jax import lax
+from jax.experimental import pallas as pl
+from jax.experimental.pallas import tpu as pltpu
 from jax.sharding import PartitionSpec as P
+
+MESH = pl.DeviceIdType.MESH
 
 score_scale = 8.0
 margin_value = 0.1
@@ -118,9 +124,377 @@
     return grad_local.at[neg_row].add(neg_rows)
 
 
+def dot(left, right, left_dim=1, right_dim=0):
+    return lax.dot_general(
+        left, right, (((left_dim,), (right_dim,)), ((), ())), preferred_element_type=jnp.float32
+    )
+
+
+def lanes_of(columns, width):
+    rows = columns[0].shape[0]
+    lane = lax.broadcasted_iota(jnp.int32, (rows, width), 1)
+    result = jnp.zeros((rows, width), jnp.float32)
+    for place, column in enumerate(columns):
+        result = jnp.where(lane == place, column, result)
+    return result
+
+
+def loss_weights(dots, stats):
+    inverse = lax.rsqrt(stats[:, 0:3] + epsilon)
+    inv_q, inv_p, inv_h = inverse[:, 0:1], inverse[:, 1:2], inverse[:, 2:3]
+    scores = dots * inv_q
+    positive = stats[:, 3:4] * inv_q * inv_p
+    hard = stats[:, 4:5] * inv_q * inv_h
+    weight = score_scale * jax.nn.sigmoid(score_scale * (scores - positive + margin_value))
+    weight = weight.astype(jnp.bfloat16)
+    wide = weight.astype(jnp.float32)
+    hard_weight = score_scale * jax.nn.sigmoid(score_scale * (hard - positive + margin_value))
+    hard_weight = hard_weight.astype(jnp.bfloat16).astype(jnp.float32)
+    total = jnp.sum(wide, axis=1, keepdims=True) + hard_weight
+    along = jnp.sum(wide * scores, axis=1, keepdims=True) + hard_weight * hard - total * positive
+    return weight, [inv_q, inv_p, inv_h, hard_weight, total, along, positive, hard]
+
+
+def query_side(hood, pos, hard, visit_total, weight, scalars, neg_slice):
+    f32, bf16 = jnp.float32, jnp.bfloat16
+    inv_q, inv_p, inv_h, hard_weight, total, along, pos_score, hard_score = [
+        scalars[:, i : i + 1] for i in range(8)
+    ]
+    query_unit, pos_unit, hard_unit = hood * inv_q, pos * inv_p, hard * inv_h
+    query_float = query_unit.astype(bf16).astype(f32)
+    query_grad = (
+        dot(weight, neg_slice)
+        + hard_weight * hard_unit.astype(bf16).astype(f32)
+        - total * pos_unit.astype(bf16).astype(f32)
+    )
+    hood_grad = (query_grad - query_unit * along) * inv_q
+    pos_grad = -total * (query_float - pos_unit * pos_score) * inv_p
+    hard_grad = hard_weight * (query_float - hard_unit * hard_score) * inv_h
+    return [hood_grad, pos_grad, hard_grad, hood_grad / visit_total], query_float
+
+
+def kernel(
+    sizes,
+    table,
+    projection,
+    info,
+    neg_column,
+    neg_line,
+    out,
+    feats,
+    pre,
+    act,
+    info_all,
+    rows,
+    slices,
+    picks,
+    picked,
+    partial,
+    parts,
+    stats,
+    stats_all,
+    weight_all,
+    scalar_all,
+    flipped,
+    back,
+    core_in,
+    across,
+    across_in,
+    turned,
+    landed,
+    pre_grad,
+    send_sem,
+    recv_sem,
+):
+    shards, slot_count, node_count, neg_count, query_count = sizes
+    f32, bf16 = jnp.float32, jnp.bfloat16
+    width = slices.shape[3]
+    embed_width = projection.shape[1]
+    node_part, neg_part = node_count // 4, neg_count // 4
+    part = node_part + neg_part
+    group = query_count * shards
+    me, rep = lax.axis_index("shard"), lax.axis_index("rep")
+    x, core = rep // 2, rep % 2
+    mine, half = 2 * core + x, 2 * core
+    crossed = 2 * core + 1 - x
+    x_peer = (me, (1 - x) * 2 + core)
+    core_peer = (me, x * 2 + 1 - core)
+    peers = [lax.rem(me + k, shards) for k in range(shards)]
+    sources = [lax.rem(me + shards - k, shards) for k in range(shards)]
+    sent = []
+
+    def send(source, target, sem, device):
+        copy = pltpu.make_async_remote_copy(
+            src_ref=source,
+            dst_ref=target,
+            send_sem=send_sem.at[sem],
+            recv_sem=recv_sem.at[sem],
+            device_id=device,
+            device_id_type=MESH,
+        )
+        copy.start()
+        sent.append(copy)
+        return copy
+
+    barrier = pltpu.get_barrier_semaphore()
+    for k in range(1, shards):
+        pl.semaphore_signal(barrier, inc=1, device_id=(peers[k], rep), device_id_type=MESH)
+    for device in (x_peer, core_peer):
+        pl.semaphore_signal(barrier, inc=1, device_id=device, device_id_type=MESH)
+
+    neg_pick = (
+        lax.broadcasted_iota(jnp.int32, (neg_count, node_count), 1) == neg_column[...]
+    ).astype(bf16)
+    neg_feat = dot(neg_pick, table[...]).astype(bf16)
+    for b in range(4):
+        feats[b * part : b * part + node_part] = table[b * node_part : (b + 1) * node_part]
+        feats[b * part + node_part : (b + 1) * part] = neg_feat[b * neg_part : (b + 1) * neg_part]
+    tile = 2 * width
+
+    def embed_tile(t, squares):
+        columns = pl.ds(pl.multiple_of(t * tile, tile), tile)
+        values = dot(feats[...], projection[:, columns])
+        pre[:, :, columns] = values.reshape(4, part, tile)
+        values = values * jax.nn.sigmoid(values)
+        act[:, :, columns] = values.reshape(4, part, tile)
+        return squares + jnp.sum(values * values, axis=1, keepdims=True)
+
+    squares = lax.fori_loop(
+        0, embed_width // tile, embed_tile, jnp.zeros((4 * part, 1), f32)
+    ).reshape(4, part, 1)
+    place = lax.broadcasted_iota(jnp.int32, (4, part, 1), 1)
+    scale = jnp.where(place >= node_part, lax.rsqrt(squares + epsilon), 1.0)
+
+    pl.semaphore_wait(barrier, shards + 1)
+
+    own_rows = pl.ds(pl.multiple_of(me * query_count, query_count), query_count)
+    info_copies = [
+        send(info, info_all.at[own_rows], k, (peers[k], rep)) for k in range(1, shards)
+    ]
+    info_all[own_rows] = info[...]
+    base = shards
+    slice_copies = []
+    for k in list(range(1, shards)) + [0]:
+        columns = pl.ds(pl.multiple_of(peers[k] * width, width), width)
+        values = (act[:, :, columns] * scale).astype(bf16)
+        if k:
+            rows[k] = values
+            slice_copies.append(
+                send(
+                    rows.at[k, pl.ds(half, 2)],
+                    slices.at[me, pl.ds(half, 2)],
+                    base + k,
+                    (peers[k], rep),
+                )
+            )
+        else:
+            slices[me] = values
+
+    for copy in info_copies:
+        copy.wait_recv()
+    block = 16
+
+    def pick_rows(step, carry):
+        start = pl.multiple_of(step * block, block)
+        ids = info_all[pl.ds(start, block)]
+        lane = lax.broadcasted_iota(jnp.int32, (block, shards * node_count), 1)
+        for s in range(3):
+            picks[s, pl.ds(start, block)] = (
+                jnp.where(lane == ids[:, s : s + 1], 1.0, 0.0).astype(bf16)
+            )
+        counts = ids.astype(f32)
+        spread = jnp.zeros(lane.shape, f32)
+        for k in range(3, slot_count):
+            spread = spread + jnp.where(
+                lane == ids[:, k : k + 1], counts[:, slot_count + k - 3 : slot_count + k - 2], 0.0
+            )
+        picks[3, pl.ds(start, block)] = spread.astype(bf16)
+        return carry
+
+    lax.fori_loop(0, group // block, pick_rows, 0)
+
+    base = 2 * shards
+    swaps = []
+    for k in range(1, shards):
+        slice_copies[k - 1].wait_recv()
+        piece = slices.at[sources[k], pl.ds(half, 2)]
+        swaps.append(send(piece, piece, base + k, core_peer))
+    for copy in swaps:
+        copy.wait_recv()
+
+    act_slice = slices[:, :, :node_part].reshape(shards * node_count, width)
+    neg_slice = slices[:, :, node_part:].reshape(shards * neg_count, width)
+
+    def pick_set(s, carry):
+        picked[s] = dot(picks[s], act_slice)
+        return carry
+
+    lax.fori_loop(0, 4, pick_set, 0)
+    counts = info_all[:, slot_count : 2 * slot_count - 3].astype(f32)
+    visit_total = jnp.sum(counts, axis=1, keepdims=True)
+    hood = picked[0] + picked[3] / visit_total
+    pos, hard = picked[1], picked[2]
+    partial[...] = dot(hood.astype(bf16), neg_slice, 1, 1).astype(bf16)
+    pairs = ((hood, hood), (pos, pos), (hard, hard), (hood, pos), (hood, hard))
+    stats[...] = lanes_of([jnp.sum(a * b, axis=1, keepdims=True) for a, b in pairs], width)
+    base = 3 * shards
+    copies = []
+    for k in range(1, shards):
+        there = pl.ds(pl.multiple_of(peers[k] * query_count, query_count), query_count)
+        copies.append(send(stats.at[there], stats_all.at[k], base + k, (peers[k], rep)))
+        copies.append(
+            send(partial.at[there], parts.at[k], base + shards + k, (peers[k], rep))
+        )
+    dots = partial[own_rows].astype(f32)
+    sums = stats[own_rows]
+    for copy in copies:
+        copy.wait_recv()
+    for k in range(1, shards):
+        dots = dots + parts[k].astype(f32)
+        sums = sums + stats_all[k]
+    weight, scalars = loss_weights(dots, sums)
+    weight_all[own_rows] = weight
+    scalar_all[own_rows] = lanes_of(scalars, width)
+    base = 5 * shards
+    copies = []
+    for k in range(1, shards):
+        there = (peers[k], rep)
+        copies.append(send(scalar_all.at[own_rows], scalar_all.at[own_rows], base + k, there))
+        copies.append(
+            send(weight_all.at[own_rows], weight_all.at[own_rows], base + shards + k, there)
+        )
+    for copy in copies:
+        copy.wait_recv()
+
+    weight = weight_all[...]
+    grads, query_float = query_side(hood, pos, hard, visit_total, weight, scalar_all[...], neg_slice)
+    for s in range(4):
+        flipped[:, s * group : (s + 1) * group] = jnp.transpose(grads[s]).astype(bf16)
+    neg_grad = jnp.transpose(dot(jnp.transpose(query_float).astype(bf16), weight))
+    back[:, :, node_part:] = neg_grad.reshape(shards, 4, neg_part, width)
+    base = 7 * shards
+    other = pl.ds(2 - half, 2)
+
+    def node_block(s, carry):
+        columns = pl.ds(pl.multiple_of(s * node_count, node_count), node_count)
+        total = jnp.zeros((width, node_count), f32)
+        for kind in range(4):
+            total = total + dot(
+                flipped[:, kind * group : (kind + 1) * group], picks[kind, :, columns]
+            )
+        back[s, :, :node_part] = jnp.transpose(total).reshape(4, node_part, width)
+        return carry
+
+    lax.fori_loop(0, shards, node_block, 0)
+    send(back.at[:, other], core_in, base, core_peer).wait_recv()
+
+    across[...] = (back[:, crossed] + core_in[:, 1 - x]).astype(bf16)
+    copy = send(across, across_in, base + 1, x_peer)
+    kept = back[:, mine] + core_in[:, x]
+    copy.wait_recv()
+    turned[...] = (kept + across_in[...].astype(f32)).astype(bf16)
+    base = 8 * shards
+    copies = [
+        send(turned.at[peers[k]], landed.at[me], base + k, (peers[k], rep))
+        for k in range(1, shards)
+    ]
+    landed[me] = turned[me]
+    for copy in copies:
+        copy.wait_recv()
+    grad = jnp.concatenate([landed[s].astype(f32) for s in range(shards)], axis=1)
+    own_pre = pre[mine]
+    neg_unit = act[mine, node_part:]
+    inverse = lax.rsqrt(jnp.sum(neg_unit * neg_unit, axis=1, keepdims=True) + epsilon)
+    neg_unit = neg_unit * inverse
+    neg_back = grad[node_part:]
+    neg_back = neg_back - neg_unit * jnp.sum(neg_unit * neg_back, axis=1, keepdims=True)
+    neg_back = neg_back * inverse
+    slope = silu_slope(own_pre)
+    pre_grad[mine, :node_part] = (grad[:node_part] * slope[:node_part]).astype(bf16)
+    pre_grad[mine, node_part:] = (neg_back * slope[node_part:]).astype(bf16)
+    base = 9 * shards
+    first = send(pre_grad.at[mine], pre_grad.at[mine], base, x_peer)
+    second = send(pre_grad.at[mine], pre_grad.at[mine], base + 1, core_peer)
+    first.wait_recv()
+    third = send(pre_grad.at[crossed], pre_grad.at[crossed], base + 2, core_peer)
+    second.wait_recv()
+    third.wait_recv()
+    node_grad = pre_grad[:, :node_part].reshape(node_count, embed_width)
+    neg_grad = pre_grad[:, node_part:].reshape(neg_count, embed_width)
+    placed = (
+        lax.broadcasted_iota(jnp.int32, (node_count, neg_count), 0) == neg_line[...]
+    ).astype(bf16)
+    out[...] = (node_grad.astype(f32) + dot(placed, neg_grad)).astype(bf16)
+    for copy in sent:
+        copy.wait_send()
+
+
+def column_split(feature_table, projection, slot_owner, slot_row, visits, neg_row):
+    shards = lax.axis_size("shard")
+    query_count, slot_count = slot_row.shape
+    node_count, feat_width = feature_table.shape
+    neg_count = neg_row.shape[0]
+    embed_width = projection.shape[1]
+    width = embed_width // shards
+    group = query_count * shards
+    part = (node_count + neg_count) // 4
+    f32, bf16 = jnp.float32, jnp.bfloat16
+    node = slot_owner.reshape(query_count, slot_count) * node_count + slot_row
+    info = jnp.concatenate([node, visits], axis=1)
+    info = jnp.pad(info, ((0, 0), (0, width - info.shape[1])))
+    sizes = (shards, slot_count, node_count, neg_count, query_count)
+    sems = 9 * shards + 3
+    vmem = pl.BlockSpec(memory_space=pltpu.VMEM)
+    pre_grad = pl.pallas_call(
+        functools.partial(kernel, sizes),
+        out_shape=jax.ShapeDtypeStruct((node_count, embed_width), bf16),
+        in_specs=[vmem] * 5,
+        out_specs=vmem,
+        scratch_shapes=[
+            pltpu.VMEM((4 * part, feat_width), bf16),
+            pltpu.VMEM((4, part, embed_width), f32),
+            pltpu.VMEM((4, part, embed_width), f32),
+            pltpu.VMEM((group, width), jnp.int32),
+            pltpu.VMEM((shards, 4, part, width), bf16),
+            pltpu.VMEM((shards, 4, part, width), bf16),
+            pltpu.VMEM((4, group, shards * node_count), bf16),
+            pltpu.VMEM((4, group, width), f32),
+            pltpu.VMEM((group, shards * neg_count), bf16),
+            pltpu.VMEM((shards, query_count, shards * neg_count), bf16),
+            pltpu.VMEM((group, width), f32),
+            pltpu.VMEM((shards, query_count, width), f32),
+            pltpu.VMEM((group, shards * neg_count), bf16),
+            pltpu.VMEM((group, width), f32),
+            pltpu.VMEM((width, 4 * group), bf16),
+            pltpu.VMEM((shards, 4, part, width), f32),
+            pltpu.VMEM((shards, 2, part, width), f32),
+            pltpu.VMEM((shards, part, width), bf16),
+            pltpu.VMEM((shards, part, width), bf16),
+            pltpu.VMEM((shards, part, width), bf16),
+            pltpu.VMEM((shards, part, width), bf16),
+            pltpu.VMEM((4, part, embed_width), bf16),
+            pltpu.SemaphoreType.DMA((sems,)),
+            pltpu.SemaphoreType.DMA((sems,)),
+        ],
+        compiler_params=pltpu.CompilerParams(
+            collective_id=0, has_side_effects=True, vmem_limit_bytes=48 * 1024 * 1024
+        ),
+    )(feature_table, projection, info, neg_row.reshape(neg_count, 1), neg_row.reshape(1, neg_count))
+    return times_back(pre_grad, projection)
+
+
 def solution(mesh):
+    shards, reps = mesh.shape["shard"], mesh.shape["rep"]
+
+    def body(feature_table, projection, slot_owner, slot_row, visits, neg_row):
+        width = projection.shape[1] // shards
+        parts = (feature_table.shape[0], neg_row.shape[0], slot_row.shape[0] * 2)
+        whole = width == 128 and reps == 4 and all(size % 64 == 0 for size in parts)
+        form = column_split if whole else on_device
+        return form(feature_table, projection, slot_owner, slot_row, visits, neg_row)
+
     return jax.shard_map(
-        on_device,
+        body,
         mesh=mesh,
         in_specs=(
             P("shard", None),

time: 275 us -> 72.8 us (0.26)
  waiting for transfers between devices: 173 us -> 0 us
  Pallas kernels: 0 us -> 64.2 us
  other arithmetic: 22.1 us -> 0.08 us
  local copies, waits for them, and re-layouts: 24.1 us -> 6.36 us
  starting transfers between devices: 15.2 us -> 0 us
  between operations: 13.4 us -> 0.02 us
  matrix products: 14.8 us -> 1.78 us
  blocking collectives: 11.5 us -> 0 us
    all_to_all x2 -> x0, waiting for transfers between devices: 112 us -> none  [the longest x1 61.1 us: on_device(): lax.all_to_all(outgoing.reshape(shard_count, capacity, embed_width), 'sha...]
    pallas_call x0 -> x1, Pallas kernels: none -> 64.2 us  [column_split(): pl.pallas_call(functools.partial(kernel, sizes), out_shape=jax.ShapeDtype...]
    psum x1 -> x0, waiting for transfers between devices: 41.8 us -> none  [on_device(): grad_local, neg_total = lax.psum((grad_local, neg_sum), 'rep')]
    reduce_scatter x1 -> x0, waiting for transfers between devices: 18.7 us -> none  [on_device(): lax.psum_scatter(neg_partial, 'shard', scatter_dimension=0, tiled=True)]
    all_to_all x2 -> x0, starting transfers between devices: 14.7 us -> none  [the longest x1 10.2 us: on_device(): lax.all_to_all(outgoing.reshape(shard_count, capacity, embed_width), 'sha...]
    scatter-add x2 -> x0, other arithmetic: 13.2 us -> none  [the longest x1 11.3 us: on_device(): grad_local = jnp.zeros((feature_table.shape[0], feat_width), jnp.float32)...]
    gather x3 -> x0, local copies, waits for them, and re-layouts: 12.5 us -> none  [the longest x1 7.17 us: on_device(): picked = feature_table[asked]]
    all_to_all x1 -> x0, blocking collectives: 11.5 us -> none  [on_device(): lax.all_to_all(send_ids, 'shard', split_axis=0, concat_axis=0, tiled=True)]
  transfers between devices with their start and end apart: 5 -> 0, of which waited for: 4 -> 0; matrix products, arithmetic and copies ran while one was open for 11% -> 0% of each run, Pallas kernels for 0% -> 0%
where the time goes in v2:
time: 72.8 us; the launch traced here: 72.5 us
  Pallas kernels  64.2 us (88%)
  local copies, waits for them, and re-layouts  6.36 us (9%)
  matrix products  1.78 us (2%)
    pallas_call x1, Pallas kernels, column_split(): pl.pallas_call(functools.partial(kernel, sizes), out_shape=jax.ShapeDtype...  64.2 us
    unnamed x9, local copies, waits for them, and re-layouts  5.6 us
    dot_general x1, matrix products, times_back(): jnp.einsum('re,fe->rf', left, projection, preferred_element_type=jnp.floa...  1.78 us

profile of v2, /device:TPU:1, one launch (start us, length us, event | category | flops | bytes accessed | tf_op | source)
XLA Modules:
  0.0 72.5 jit_solution(7563562364864822472)
XLA Ops:
  0.0 0.8 %copy.7 = s32[32,16,1]{1,0,2:T(8,128)S(1)} copy(s32[32,16,1]{0,2,1:T(1,128)} %param.8) | data formatting | bytes 4096 | tf_op args[2]
  0.8 0.8 %copy.8 = s32[32,16]{1,0:T(8,128)S(1)} copy(s32[32,16]{0,1:T(8,128)} %param.9) | data formatting | bytes 4096 | tf_op args[3]
  1.5 0.8 %copy.9 = s32[32,13]{1,0:T(8,128)S(1)} copy(s32[32,13]{0,1:T(8,128)} %param.10) | data formatting | bytes 3328 | tf_op args[4]
  2.3 0.1 pad_add_fusion
  2.4 0.7 %copy.10.neg_column = s32[64,1]{1,0:T(8,128)S(1)} copy(s32[64,1]{0,1:T(1,128)} %bitcast.6) | data formatting | bytes 512 | tf_op jit(solution)/shard_map/reshape | solution.py:482
  3.2 0.0 copy-start
  3.2 1.6 %copy-done = bf16[1024,1024]{1,0:T(8,128)(2,1)S(1)} copy-done((bf16[1024,1024]{1,0:T(8,128)(2,1)S(1)}, bf16[1024,1024]{1,0:T(8,128)(2,1)}, u32[]{:S(2)}) %copy-start) | copy-done | bytes 2097176
  4.8 0.0 copy-start.1
  4.8 1.0 %copy-done.1 = bf16[256,1024]{1,0:T(8,128)(2,1)S(1)} copy-done((bf16[256,1024]{1,0:T(8,128)(2,1)S(1)}, bf16[256,1024]{1,0:T(8,128)(2,1)}, u32[]{:S(2)}) %copy-start.1) | copy-done | bytes 524312
  5.8 0.0 copy-start.2
  5.8 0.7 copy-done.2
  6.4 64.2 %shard_map.64 = bf16[256,1024]{1,0:T(8,128)(2,1)S(1)} custom-call(bf16[256,1024]{1,0:T(8,128)(2,1)S(1)} %copy-done.1, bf16[1024,1024]{1,0:T(8,128)(2,1)S(1)} %copy-done, s32[32,128]{1,0:T(8,128)S(1)} %pad.4.info, s32[64,1]{1,0:T(8,128)S(1)} %copy.10.neg_column, s32[1,64]{1,0:T(1,128)S(1)} %bitcast.7), custom_call_target="tpu_custom_call" | custom-call | tf_op jit(solution)/shard_map/pallas_call | solution.py:448
  70.7 1.8 %fusion = f32[256,1024]{1,0:T(8,128)} fusion(bf16[256,1024]{1,0:T(8,128)(2,1)S(1)} %shard_map.64, bf16[1024,1024]{1,0:T(8,128)(2,1)S(1)} %copy-done), kind=kOutput, calls=%fused_computation.2 | convolution fusion | flops 536870912 | bytes 3670016 | tf_op jit(solution)/shard_map/re,fe->rf/dot_general | solution.py:32
  (2 shorter events, 0.0 us)
Async XLA Ops:
  3.2 1.6 %copy-start = (bf16[1024,1024]{1,0:T(8,128)(2,1)S(1)}, bf16[1024,1024]{1,0:T(8,128)(2,1)}, u32[]{:S(2)}) copy-start(bf16[1024,1024]{1,0:T(8,128)(2,1)} %projection.1) | copy-start | bytes 6291460
  4.8 1.0 %copy-start.1 = (bf16[256,1024]{1,0:T(8,128)(2,1)S(1)}, bf16[256,1024]{1,0:T(8,128)(2,1)}, u32[]{:S(2)}) copy-start(bf16[256,1024]{1,0:T(8,128)(2,1)} %table.1) | copy-start | bytes 1572868
  5.8 0.7 copy-start.2

commit v3 on v2

--- a/solution.py
+++ b/solution.py
@@ -155,32 +155,36 @@
     return weight, [inv_q, inv_p, inv_h, hard_weight, total, along, positive, hard]
 
 
-def query_side(hood, pos, hard, visit_total, weight, scalars, neg_slice):
+def item_side(hood, pos, hard, scalars):
     f32, bf16 = jnp.float32, jnp.bfloat16
     inv_q, inv_p, inv_h, hard_weight, total, along, pos_score, hard_score = [
         scalars[:, i : i + 1] for i in range(8)
     ]
     query_unit, pos_unit, hard_unit = hood * inv_q, pos * inv_p, hard * inv_h
     query_float = query_unit.astype(bf16).astype(f32)
-    query_grad = (
-        dot(weight, neg_slice)
-        + hard_weight * hard_unit.astype(bf16).astype(f32)
-        - total * pos_unit.astype(bf16).astype(f32)
-    )
-    hood_grad = (query_grad - query_unit * along) * inv_q
+    known_grad = hard_weight * hard_unit.astype(bf16).astype(
+        f32
+    ) - total * pos_unit.astype(bf16).astype(f32)
     pos_grad = -total * (query_float - pos_unit * pos_score) * inv_p
     hard_grad = hard_weight * (query_float - hard_unit * hard_score) * inv_h
-    return [hood_grad, pos_grad, hard_grad, hood_grad / visit_total], query_float
+    return query_unit, query_float, known_grad, pos_grad, hard_grad
 
 
 def kernel(
     sizes,
+    table_hbm,
+    projection_hbm,
+    owner_line,
+    row_line,
+    visit_line,
+    neg_line,
+    out,
     table,
     projection,
+    lines,
     info,
-    neg_column,
-    neg_line,
-    out,
+    slope,
+    early,
     feats,
     pre,
     act,
@@ -205,11 +209,12 @@
     pre_grad,
     send_sem,
     recv_sem,
+    local_sem,
 ):
     shards, slot_count, node_count, neg_count, query_count = sizes
     f32, bf16 = jnp.float32, jnp.bfloat16
     width = slices.shape[3]
-    embed_width = projection.shape[1]
+    embed_width = projection_hbm.shape[1]
     node_part, neg_part = node_count // 4, neg_count // 4
     part = node_part + neg_part
     group = query_count * shards
@@ -222,6 +227,18 @@
     peers = [lax.rem(me + k, shards) for k in range(shards)]
     sources = [lax.rem(me + shards - k, shards) for k in range(shards)]
     sent = []
+    tile = 2 * width
+    tiles = embed_width // tile
+    loads = [pltpu.make_async_copy(table_hbm, table, local_sem.at[tiles])]
+    for t in range(tiles):
+        columns = pl.ds(t * tile, tile)
+        loads.append(
+            pltpu.make_async_copy(
+                projection_hbm.at[:, columns], projection.at[t], local_sem.at[t]
+            )
+        )
+    for load in loads:
+        load.start()
 
     def send(source, target, sem, device):
         copy = pltpu.make_async_remote_copy(
@@ -242,26 +259,32 @@
     for device in (x_peer, core_peer):
         pl.semaphore_signal(barrier, inc=1, device_id=device, device_id_type=MESH)
 
+    lines[...] = jnp.zeros(lines.shape, f32)
+    lines[0:slot_count, 0:query_count] = (
+        owner_line[...] * node_count + row_line[...]
+    ).astype(f32)
+    lines[slot_count : 2 * slot_count - 3, 0:query_count] = visit_line[...].astype(f32)
+    lines[2 * slot_count : 2 * slot_count + 1, 0:neg_count] = neg_line[...].astype(f32)
+    columns = jnp.transpose(lines[...])
+    info[...] = columns[0:query_count]
+    neg_column = columns[0:neg_count, 2 * slot_count : 2 * slot_count + 1].astype(jnp.int32)
     neg_pick = (
-        lax.broadcasted_iota(jnp.int32, (neg_count, node_count), 1) == neg_column[...]
+        lax.broadcasted_iota(jnp.int32, (neg_count, node_count), 1) == neg_column
     ).astype(bf16)
+    loads[0].wait()
     neg_feat = dot(neg_pick, table[...]).astype(bf16)
     for b in range(4):
         feats[b * part : b * part + node_part] = table[b * node_part : (b + 1) * node_part]
         feats[b * part + node_part : (b + 1) * part] = neg_feat[b * neg_part : (b + 1) * neg_part]
-    tile = 2 * width
-
-    def embed_tile(t, squares):
-        columns = pl.ds(pl.multiple_of(t * tile, tile), tile)
-        values = dot(feats[...], projection[:, columns])
-        pre[:, :, columns] = values.reshape(4, part, tile)
+    squares = jnp.zeros((4 * part, 1), f32)
+    for t in range(tiles):
+        loads[1 + t].wait()
+        values = dot(feats[...], projection[t])
+        pre[:, :, t * tile : (t + 1) * tile] = values.reshape(4, part, tile)
         values = values * jax.nn.sigmoid(values)
-        act[:, :, columns] = values.reshape(4, part, tile)
-        return squares + jnp.sum(values * values, axis=1, keepdims=True)
-
-    squares = lax.fori_loop(
-        0, embed_width // tile, embed_tile, jnp.zeros((4 * part, 1), f32)
-    ).reshape(4, part, 1)
+        act[:, :, t * tile : (t + 1) * tile] = values.reshape(4, part, tile)
+        squares = squares + jnp.sum(values * values, axis=1, keepdims=True)
+    squares = squares.reshape(4, part, 1)
     place = lax.broadcasted_iota(jnp.int32, (4, part, 1), 1)
     scale = jnp.where(place >= node_part, lax.rsqrt(squares + epsilon), 1.0)
 
@@ -297,12 +320,12 @@
     def pick_rows(step, carry):
         start = pl.multiple_of(step * block, block)
         ids = info_all[pl.ds(start, block)]
-        lane = lax.broadcasted_iota(jnp.int32, (block, shards * node_count), 1)
+        lane = lax.broadcasted_iota(jnp.int32, (block, shards * node_count), 1).astype(f32)
         for s in range(3):
             picks[s, pl.ds(start, block)] = (
                 jnp.where(lane == ids[:, s : s + 1], 1.0, 0.0).astype(bf16)
             )
-        counts = ids.astype(f32)
+        counts = ids
         spread = jnp.zeros(lane.shape, f32)
         for k in range(3, slot_count):
             spread = spread + jnp.where(
@@ -313,24 +336,28 @@
 
     lax.fori_loop(0, group // block, pick_rows, 0)
 
+    def gather_from(k, first=False):
+        source = sources[k]
+        columns = pl.ds(pl.multiple_of(source * node_count, node_count), node_count)
+        values = slices[source, :, :node_part].reshape(node_count, width)
+        for kind in range(4):
+            part_sum = dot(picks[kind, :, columns], values)
+            picked[kind] = part_sum if first else picked[kind] + part_sum
+
     base = 2 * shards
     swaps = []
+    gather_from(0, True)
     for k in range(1, shards):
         slice_copies[k - 1].wait_recv()
         piece = slices.at[sources[k], pl.ds(half, 2)]
         swaps.append(send(piece, piece, base + k, core_peer))
-    for copy in swaps:
-        copy.wait_recv()
-
-    act_slice = slices[:, :, :node_part].reshape(shards * node_count, width)
+        if k > 1:
+            swaps[k - 2].wait_recv()
+            gather_from(k - 1)
+    swaps[shards - 2].wait_recv()
+    gather_from(shards - 1)
     neg_slice = slices[:, :, node_part:].reshape(shards * neg_count, width)
-
-    def pick_set(s, carry):
-        picked[s] = dot(picks[s], act_slice)
-        return carry
-
-    lax.fori_loop(0, 4, pick_set, 0)
-    counts = info_all[:, slot_count : 2 * slot_count - 3].astype(f32)
+    counts = info_all[:, slot_count : 2 * slot_count - 3]
     visit_total = jnp.sum(counts, axis=1, keepdims=True)
     hood = picked[0] + picked[3] / visit_total
     pos, hard = picked[1], picked[2]
@@ -345,6 +372,10 @@
         copies.append(
             send(partial.at[there], parts.at[k], base + shards + k, (peers[k], rep))
         )
+    slope[...] = silu_slope(pre[mine])
+    neg_unit = act[mine, node_part:]
+    inverse = lax.rsqrt(jnp.sum(neg_unit * neg_unit, axis=1, keepdims=True) + epsilon)
+    neg_unit = neg_unit * inverse
     dots = partial[own_rows].astype(f32)
     sums = stats[own_rows]
     for copy in copies:
@@ -356,75 +387,117 @@
     weight_all[own_rows] = weight
     scalar_all[own_rows] = lanes_of(scalars, width)
     base = 5 * shards
-    copies = []
-    for k in range(1, shards):
-        there = (peers[k], rep)
-        copies.append(send(scalar_all.at[own_rows], scalar_all.at[own_rows], base + k, there))
-        copies.append(
-            send(weight_all.at[own_rows], weight_all.at[own_rows], base + shards + k, there)
-        )
+    copies = [
+        send(scalar_all.at[own_rows], scalar_all.at[own_rows], base + k, (peers[k], rep))
+        for k in range(1, shards)
+    ]
+    weight_copies = [
+        send(weight_all.at[own_rows], weight_all.at[own_rows], base + shards + k, (peers[k], rep))
+        for k in range(1, shards)
+    ]
     for copy in copies:
         copy.wait_recv()
+    scalars = scalar_all[...]
+    side = item_side(hood, pos, hard, scalars)
+    query_unit, query_float, known_grad, pos_grad, hard_grad = side
+    flipped[:, 0:group] = jnp.transpose(pos_grad).astype(bf16)
+    flipped[:, group : 2 * group] = jnp.transpose(hard_grad).astype(bf16)
+    query_flipped = jnp.transpose(query_float).astype(bf16)
+
+    def early_block(s, carry):
+        columns = pl.ds(pl.multiple_of(s * node_count, node_count), node_count)
+        early[s] = dot(flipped[:, 0:group], picks[1, :, columns]) + dot(
+            flipped[:, group : 2 * group], picks[2, :, columns]
+        )
+        return carry
+
+    lax.fori_loop(0, shards, early_block, 0)
+    for copy in weight_copies:
+        copy.wait_recv()
 
     weight = weight_all[...]
-    grads, query_float = query_side(hood, pos, hard, visit_total, weight, scalar_all[...], neg_slice)
-    for s in range(4):
-        flipped[:, s * group : (s + 1) * group] = jnp.transpose(grads[s]).astype(bf16)
-    neg_grad = jnp.transpose(dot(jnp.transpose(query_float).astype(bf16), weight))
+    along, inv_q = scalars[:, 5:6], scalars[:, 0:1]
+    hood_grad = (dot(weight, neg_slice) + known_grad - query_unit * along) * inv_q
+    flipped[:, 2 * group : 3 * group] = jnp.transpose(hood_grad).astype(bf16)
+    flipped[:, 3 * group :] = jnp.transpose(hood_grad / visit_total).astype(bf16)
+    neg_grad = jnp.transpose(dot(query_flipped, weight))
     back[:, :, node_part:] = neg_grad.reshape(shards, 4, neg_part, width)
-    base = 7 * shards
     other = pl.ds(2 - half, 2)
-
-    def node_block(s, carry):
+    order = list(range(1, shards)) + [0]
+    core_copies, x_copies, row_copies = {}, {}, {}
+
+    def to_core(k):
+        s = peers[k]
         columns = pl.ds(pl.multiple_of(s * node_count, node_count), node_count)
-        total = jnp.zeros((width, node_count), f32)
-        for kind in range(4):
-            total = total + dot(
-                flipped[:, kind * group : (kind + 1) * group], picks[kind, :, columns]
-            )
+        total = early[s] + dot(flipped[:, 2 * group : 3 * group], picks[0, :, columns])
+        total = total + dot(flipped[:, 3 * group :], picks[3, :, columns])
         back[s, :, :node_part] = jnp.transpose(total).reshape(4, node_part, width)
-        return carry
-
-    lax.fori_loop(0, shards, node_block, 0)
-    send(back.at[:, other], core_in, base, core_peer).wait_recv()
-
-    across[...] = (back[:, crossed] + core_in[:, 1 - x]).astype(bf16)
-    copy = send(across, across_in, base + 1, x_peer)
-    kept = back[:, mine] + core_in[:, x]
-    copy.wait_recv()
-    turned[...] = (kept + across_in[...].astype(f32)).astype(bf16)
-    base = 8 * shards
-    copies = [
-        send(turned.at[peers[k]], landed.at[me], base + k, (peers[k], rep))
-        for k in range(1, shards)
-    ]
-    landed[me] = turned[me]
-    for copy in copies:
-        copy.wait_recv()
-    grad = jnp.concatenate([landed[s].astype(f32) for s in range(shards)], axis=1)
-    own_pre = pre[mine]
-    neg_unit = act[mine, node_part:]
-    inverse = lax.rsqrt(jnp.sum(neg_unit * neg_unit, axis=1, keepdims=True) + epsilon)
-    neg_unit = neg_unit * inverse
-    neg_back = grad[node_part:]
+        core_copies[k] = send(back.at[s, other], core_in.at[s], 7 * shards + k, core_peer)
+
+    def to_x(k):
+        s = peers[k]
+        core_copies[k].wait_recv()
+        across[s] = (back[s, crossed] + core_in[s, 1 - x]).astype(bf16)
+        x_copies[k] = send(across.at[s], across_in.at[s], 8 * shards + k, x_peer)
+
+    def to_holder(k):
+        s = peers[k]
+        x_copies[k].wait_recv()
+        total = back[s, mine] + core_in[s, x] + across_in[s].astype(f32)
+        if k:
+            turned[k] = total.astype(bf16)
+            row_copies[k] = send(turned.at[k], landed.at[me], 9 * shards + k, (s, rep))
+        else:
+            landed[me] = total.astype(bf16)
+
+    lag = 3
+    for step in range(shards + lag):
+        if step < shards:
+            to_core(order[step])
+        if step >= lag:
+            to_x(order[step - lag])
+    for k in order:
+        to_holder(k)
+
+    home = [0] + list(range(1, shards))
+    to_x_peer, to_core_peer, passed = [], [], []
+    for k in home:
+        if k:
+            row_copies[k].wait_recv()
+        s = sources[k]
+        columns = pl.ds(pl.multiple_of(s * width, width), width)
+        values = landed[s, :node_part].astype(f32) * slope[:node_part, columns]
+        pre_grad[s, mine, :node_part] = values.astype(bf16)
+        piece = pre_grad.at[s, mine, pl.ds(0, node_part)]
+        to_x_peer.append(send(piece, piece, 10 * shards + k, x_peer))
+        to_core_peer.append(send(piece, piece, 11 * shards + k, core_peer))
+    neg_back = jnp.concatenate(
+        [landed[s, node_part:].astype(f32) for s in range(shards)], axis=1
+    )
     neg_back = neg_back - neg_unit * jnp.sum(neg_unit * neg_back, axis=1, keepdims=True)
-    neg_back = neg_back * inverse
-    slope = silu_slope(own_pre)
-    pre_grad[mine, :node_part] = (grad[:node_part] * slope[:node_part]).astype(bf16)
-    pre_grad[mine, node_part:] = (neg_back * slope[node_part:]).astype(bf16)
-    base = 9 * shards
-    first = send(pre_grad.at[mine], pre_grad.at[mine], base, x_peer)
-    second = send(pre_grad.at[mine], pre_grad.at[mine], base + 1, core_peer)
-    first.wait_recv()
-    third = send(pre_grad.at[crossed], pre_grad.at[crossed], base + 2, core_peer)
-    second.wait_recv()
-    third.wait_recv()
-    node_grad = pre_grad[:, :node_part].reshape(node_count, embed_width)
-    neg_grad = pre_grad[:, node_part:].reshape(neg_count, embed_width)
+    neg_back = (neg_back * inverse * slope[node_part:]).astype(bf16)
+    for s in range(shards):
+        pre_grad[s, mine, node_part:] = neg_back[:, s * width : (s + 1) * width]
+    piece = pre_grad.at[:, mine, pl.ds(node_part, neg_part)]
+    last = 13 * shards
+    to_x_peer.append(send(piece, piece, last, x_peer))
+    to_core_peer.append(send(piece, piece, last + 1, core_peer))
+    for k in home:
+        to_x_peer[k].wait_recv()
+        piece = pre_grad.at[sources[k], crossed, pl.ds(0, node_part)]
+        passed.append(send(piece, piece, 12 * shards + k, core_peer))
+    to_x_peer[shards].wait_recv()
+    piece = pre_grad.at[:, crossed, pl.ds(node_part, neg_part)]
+    passed.append(send(piece, piece, last + 2, core_peer))
     placed = (
         lax.broadcasted_iota(jnp.int32, (node_count, neg_count), 0) == neg_line[...]
     ).astype(bf16)
-    out[...] = (node_grad.astype(f32) + dot(placed, neg_grad)).astype(bf16)
+    for copy in to_core_peer + passed:
+        copy.wait_recv()
+    for s in range(shards):
+        node_grad = pre_grad[s, :, :node_part].reshape(node_count, width).astype(f32)
+        neg_grad = pre_grad[s, :, node_part:].reshape(neg_count, width)
+        out[:, s * width : (s + 1) * width] = (node_grad + dot(placed, neg_grad)).astype(bf16)
     for copy in sent:
         copy.wait_send()
 
@@ -439,22 +512,28 @@
     group = query_count * shards
     part = (node_count + neg_count) // 4
     f32, bf16 = jnp.float32, jnp.bfloat16
-    node = slot_owner.reshape(query_count, slot_count) * node_count + slot_row
-    info = jnp.concatenate([node, visits], axis=1)
-    info = jnp.pad(info, ((0, 0), (0, width - info.shape[1])))
+    owner_line = jnp.transpose(slot_owner, (1, 2, 0)).reshape(slot_count, query_count)
     sizes = (shards, slot_count, node_count, neg_count, query_count)
-    sems = 9 * shards + 3
+    sems = 13 * shards + 3
+    tiles = embed_width // (2 * width)
+    hbm = pl.BlockSpec(memory_space=pl.ANY)
     vmem = pl.BlockSpec(memory_space=pltpu.VMEM)
     pre_grad = pl.pallas_call(
         functools.partial(kernel, sizes),
         out_shape=jax.ShapeDtypeStruct((node_count, embed_width), bf16),
-        in_specs=[vmem] * 5,
+        in_specs=[hbm] * 2 + [vmem] * 4,
         out_specs=vmem,
         scratch_shapes=[
+            pltpu.VMEM((node_count, feat_width), bf16),
+            pltpu.VMEM((tiles, feat_width, 2 * width), bf16),
+            pltpu.VMEM((128, 128), f32),
+            pltpu.VMEM((query_count, width), f32),
+            pltpu.VMEM((part, embed_width), f32),
+            pltpu.VMEM((shards, width, node_count), f32),
             pltpu.VMEM((4 * part, feat_width), bf16),
             pltpu.VMEM((4, part, embed_width), f32),
             pltpu.VMEM((4, part, embed_width), f32),
-            pltpu.VMEM((group, width), jnp.int32),
+            pltpu.VMEM((group, width), f32),
             pltpu.VMEM((shards, 4, part, width), bf16),
             pltpu.VMEM((shards, 4, part, width), bf16),
             pltpu.VMEM((4, group, shards * node_count), bf16),
@@ -472,14 +551,22 @@
             pltpu.VMEM((shards, part, width), bf16),
             pltpu.VMEM((shards, part, width), bf16),
             pltpu.VMEM((shards, part, width), bf16),
-            pltpu.VMEM((4, part, embed_width), bf16),
+            pltpu.VMEM((shards, 4, part, width), bf16),
             pltpu.SemaphoreType.DMA((sems,)),
             pltpu.SemaphoreType.DMA((sems,)),
+            pltpu.SemaphoreType.DMA((tiles + 1,)),
         ],
         compiler_params=pltpu.CompilerParams(
-            collective_id=0, has_side_effects=True, vmem_limit_bytes=48 * 1024 * 1024
+            collective_id=0, has_side_effects=True, vmem_limit_bytes=60 * 1024 * 1024
         ),
-    )(feature_table, projection, info, neg_row.reshape(neg_count, 1), neg_row.reshape(1, neg_count))
+    )(
+        feature_table,
+        projection,
+        owner_line,
+        jnp.transpose(slot_row),
+        jnp.transpose(visits),
+        neg_row.reshape(1, neg_count),
+    )
     return times_back(pre_grad, projection)
 
 
@@ -489,7 +576,8 @@
     def body(feature_table, projection, slot_owner, slot_row, visits, neg_row):
         width = projection.shape[1] // shards
         parts = (feature_table.shape[0], neg_row.shape[0], slot_row.shape[0] * 2)
-        whole = width == 128 and reps == 4 and all(size % 64 == 0 for size in parts)
+        small = slot_row.shape[0] <= 128 and neg_row.shape[0] <= 128 and slot_row.shape[1] <= 32
+        whole = width == 128 and reps == 4 and small and all(size % 64 == 0 for size in parts)
         form = column_split if whole else on_device
         return form(feature_table, projection, slot_owner, slot_row, visits, neg_row)
 

time: 72.8 us -> 68.6 us (0.942)
  local copies, waits for them, and re-layouts: 6.36 us -> 0.01 us
  Pallas kernels: 64.2 us -> 65.6 us
  matrix products: 1.78 us -> 2.76 us
    unnamed x9 -> x2, local copies, waits for them, and re-layouts: 5.6 us -> 0.01 us
    pallas_call x1, Pallas kernels: 64.2 us -> 65.6 us  [column_split(): pl.pallas_call(functools.partial(kernel, sizes), out_shape=jax.ShapeDtype...]
    dot_general x1, matrix products: 1.78 us -> 2.76 us  [times_back(): jnp.einsum('re,fe->rf', left, projection, preferred_element_type=jnp.floa...]
    reshape x1 -> x0, local copies, waits for them, and re-layouts: 0.75 us -> none  [column_split(): neg_row.reshape(neg_count, 1)]
where the time goes in v3:
time: 68.6 us; the launch traced here: 68.4 us
  Pallas kernels  65.6 us (96%)
  matrix products  2.76 us (4%)
    pallas_call x1, Pallas kernels, column_split(): pl.pallas_call(functools.partial(kernel, sizes), out_shape=jax.ShapeDtype...  65.6 us
    dot_general x1, matrix products, times_back(): jnp.einsum('re,fe->rf', left, projection, preferred_element_type=jnp.floa...  2.76 us

profile of v3, /device:TPU:1, one launch (start us, length us, event | category | flops | bytes accessed | tf_op | source)
XLA Modules:
  0.0 68.4 jit_solution(11943181063324790382)
XLA Ops:
  0.0 0.0 copy-start
  0.0 65.6 %shard_map.64 = bf16[256,1024]{1,0:T(8,128)(2,1)} custom-call(bf16[256,1024]{1,0:T(8,128)(2,1)} %table_hbm.1, bf16[1024,1024]{1,0:T(8,128)(2,1)} %projection_hbm.1, s32[16,32]{1,0:T(8,128)} %bitcast.10, s32[16,32]{1,0:T(8,128)} %bitcast.11, s32[13,32]{1,0:T(8,128)} %bitcast.12, s32[1,64]{1,0:T(1,128)} %bitcast.13), custom_call_target="tpu_custom_call" | custom-call | tf_op jit(solution)/shard_map/pallas_call | solution.py:521
  65.7 0.0 copy-done
  65.7 2.8 %fusion = f32[256,1024]{1,0:T(8,128)} fusion(bf16[256,1024]{1,0:T(8,128)(2,1)} %shard_map.64, bf16[1024,1024]{1,0:T(8,128)(2,1)S(1)} %copy-done), kind=kOutput, calls=%fused_computation | convolution fusion | flops 536870912 | bytes 3670016 | tf_op jit(solution)/shard_map/re,fe->rf/dot_general | solution.py:32
Async XLA Ops:
  0.0 65.7 %copy-start = (bf16[1024,1024]{1,0:T(8,128)(2,1)S(1)}, bf16[1024,1024]{1,0:T(8,128)(2,1)}, u32[]{:S(2)}) copy-start(bf16[1024,1024]{1,0:T(8,128)(2,1)} %projection_hbm.1) | copy-start | bytes 6291460

commit v4 on v3

--- a/solution.py
+++ b/solution.py
@@ -185,6 +185,7 @@
     info,
     slope,
     early,
+    summed,
     feats,
     pre,
     act,
@@ -240,7 +241,8 @@
     for load in loads:
         load.start()
 
-    def send(source, target, sem, device):
+    def send(source, target, device):
+        sem = len(sent)
         copy = pltpu.make_async_remote_copy(
             src_ref=source,
             dst_ref=target,
@@ -292,7 +294,7 @@
 
     own_rows = pl.ds(pl.multiple_of(me * query_count, query_count), query_count)
     info_copies = [
-        send(info, info_all.at[own_rows], k, (peers[k], rep)) for k in range(1, shards)
+        send(info, info_all.at[own_rows], (peers[k], rep)) for k in range(1, shards)
     ]
     info_all[own_rows] = info[...]
     base = shards
@@ -303,12 +305,7 @@
         if k:
             rows[k] = values
             slice_copies.append(
-                send(
-                    rows.at[k, pl.ds(half, 2)],
-                    slices.at[me, pl.ds(half, 2)],
-                    base + k,
-                    (peers[k], rep),
-                )
+                send(rows.at[k, mine], slices.at[me, mine], (peers[k], rep))
             )
         else:
             slices[me] = values
@@ -334,28 +331,44 @@
         picks[3, pl.ds(start, block)] = spread.astype(bf16)
         return carry
 
-    lax.fori_loop(0, group // block, pick_rows, 0)
-
-    def gather_from(k, first=False):
+    over_x, over_core, twice = {}, {}, {}
+
+    def pass_on(k):
+        slice_copies[k - 1].wait_recv()
+        piece = slices.at[sources[k], mine]
+        over_x[k] = send(piece, piece, x_peer)
+        over_core[k] = send(piece, piece, core_peer)
+
+    def pass_twice(k):
+        over_x[k].wait_recv()
+        piece = slices.at[sources[k], crossed]
+        twice[k] = send(piece, piece, core_peer)
+
+    def gather_from(k):
         source = sources[k]
+        if k:
+            over_core[k].wait_recv()
+            twice[k].wait_recv()
         columns = pl.ds(pl.multiple_of(source * node_count, node_count), node_count)
         values = slices[source, :, :node_part].reshape(node_count, width)
         for kind in range(4):
             part_sum = dot(picks[kind, :, columns], values)
-            picked[kind] = part_sum if first else picked[kind] + part_sum
-
-    base = 2 * shards
-    swaps = []
-    gather_from(0, True)
-    for k in range(1, shards):
-        slice_copies[k - 1].wait_recv()
-        piece = slices.at[sources[k], pl.ds(half, 2)]
-        swaps.append(send(piece, piece, base + k, core_peer))
-        if k > 1:
-            swaps[k - 2].wait_recv()
-            gather_from(k - 1)
-    swaps[shards - 2].wait_recv()
-    gather_from(shards - 1)
+            picked[kind] = picked[kind] + part_sum if k else part_sum
+
+    steps = group // block
+    last = shards - 1
+    lax.fori_loop(0, steps // 2, pick_rows, 0)
+    for k in range(1, shards // 2):
+        pass_on(k)
+    lax.fori_loop(steps // 2, steps - steps // 4, pick_rows, 0)
+    for k in range(shards // 2, shards):
+        pass_on(k)
+        pass_twice(k - shards // 2 + 1)
+    lax.fori_loop(steps - steps // 4, steps, pick_rows, 0)
+    for k in range(shards):
+        if k + shards // 2 < last:
+            pass_twice(k + shards // 2 + 1)
+        gather_from(k)
     neg_slice = slices[:, :, node_part:].reshape(shards * neg_count, width)
     counts = info_all[:, slot_count : 2 * slot_count - 3]
     visit_total = jnp.sum(counts, axis=1, keepdims=True)
@@ -363,38 +376,56 @@
     pos, hard = picked[1], picked[2]
     partial[...] = dot(hood.astype(bf16), neg_slice, 1, 1).astype(bf16)
     pairs = ((hood, hood), (pos, pos), (hard, hard), (hood, pos), (hood, hard))
+    part_rows = query_count // 2
+
+    def half_rows(owner, h):
+        start = owner * query_count + h * part_rows
+        return pl.ds(pl.multiple_of(start, part_rows), part_rows)
+
+    def send_half(h):
+        there = pl.ds(h * part_rows, part_rows)
+        return [
+            send(partial.at[half_rows(peers[k], h)], parts.at[k, there], (peers[k], rep))
+            for k in range(1, shards)
+        ]
+
+    score_copies = [send_half(0)]
     stats[...] = lanes_of([jnp.sum(a * b, axis=1, keepdims=True) for a, b in pairs], width)
-    base = 3 * shards
-    copies = []
+    stat_copies = []
     for k in range(1, shards):
         there = pl.ds(pl.multiple_of(peers[k] * query_count, query_count), query_count)
-        copies.append(send(stats.at[there], stats_all.at[k], base + k, (peers[k], rep)))
-        copies.append(
-            send(partial.at[there], parts.at[k], base + shards + k, (peers[k], rep))
-        )
+        stat_copies.append(send(stats.at[there], stats_all.at[k], (peers[k], rep)))
+    score_copies.append(send_half(1))
     slope[...] = silu_slope(pre[mine])
     neg_unit = act[mine, node_part:]
     inverse = lax.rsqrt(jnp.sum(neg_unit * neg_unit, axis=1, keepdims=True) + epsilon)
     neg_unit = neg_unit * inverse
-    dots = partial[own_rows].astype(f32)
     sums = stats[own_rows]
-    for copy in copies:
+    for copy in stat_copies:
         copy.wait_recv()
     for k in range(1, shards):
-        dots = dots + parts[k].astype(f32)
         sums = sums + stats_all[k]
-    weight, scalars = loss_weights(dots, sums)
-    weight_all[own_rows] = weight
-    scalar_all[own_rows] = lanes_of(scalars, width)
-    base = 5 * shards
-    copies = [
-        send(scalar_all.at[own_rows], scalar_all.at[own_rows], base + k, (peers[k], rep))
-        for k in range(1, shards)
-    ]
-    weight_copies = [
-        send(weight_all.at[own_rows], weight_all.at[own_rows], base + shards + k, (peers[k], rep))
-        for k in range(1, shards)
-    ]
+    weight_copies, copies = [], []
+    for h in range(2):
+        there = half_rows(me, h)
+        dots = partial[there].astype(f32)
+        for copy in score_copies[h]:
+            copy.wait_recv()
+        held = slice(h * part_rows, (h + 1) * part_rows)
+        for k in range(1, shards):
+            dots = dots + parts[k, held].astype(f32)
+        weight, scalars = loss_weights(dots, sums[held])
+        weight_all[there] = weight
+        scalar_all[there] = lanes_of(scalars, width)
+        if h:
+            copies = [
+                send(scalar_all.at[own_rows], scalar_all.at[own_rows], (peers[k], rep))
+                for k in range(1, shards)
+            ]
+        for k in range(1, shards):
+            weight_copies.append(
+                send(weight_all.at[there], weight_all.at[there], (peers[k], rep))
+            )
     for copy in copies:
         copy.wait_recv()
     scalars = scalar_all[...]
@@ -432,13 +463,13 @@
         total = early[s] + dot(flipped[:, 2 * group : 3 * group], picks[0, :, columns])
         total = total + dot(flipped[:, 3 * group :], picks[3, :, columns])
         back[s, :, :node_part] = jnp.transpose(total).reshape(4, node_part, width)
-        core_copies[k] = send(back.at[s, other], core_in.at[s], 7 * shards + k, core_peer)
+        core_copies[k] = send(back.at[s, other], core_in.at[s], core_peer)
 
     def to_x(k):
         s = peers[k]
         core_copies[k].wait_recv()
         across[s] = (back[s, crossed] + core_in[s, 1 - x]).astype(bf16)
-        x_copies[k] = send(across.at[s], across_in.at[s], 8 * shards + k, x_peer)
+        x_copies[k] = send(across.at[s], across_in.at[s], x_peer)
 
     def to_holder(k):
         s = peers[k]
@@ -446,7 +477,7 @@
         total = back[s, mine] + core_in[s, x] + across_in[s].astype(f32)
         if k:
             turned[k] = total.astype(bf16)
-            row_copies[k] = send(turned.at[k], landed.at[me], 9 * shards + k, (s, rep))
+            row_copies[k] = send(turned.at[k], landed.at[me], (s, rep))
         else:
             landed[me] = total.astype(bf16)
 
@@ -469,8 +500,8 @@
         values = landed[s, :node_part].astype(f32) * slope[:node_part, columns]
         pre_grad[s, mine, :node_part] = values.astype(bf16)
         piece = pre_grad.at[s, mine, pl.ds(0, node_part)]
-        to_x_peer.append(send(piece, piece, 10 * shards + k, x_peer))
-        to_core_peer.append(send(piece, piece, 11 * shards + k, core_peer))
+        to_x_peer.append(send(piece, piece, x_peer))
+        to_core_peer.append(send(piece, piece, core_peer))
     neg_back = jnp.concatenate(
         [landed[s, node_part:].astype(f32) for s in range(shards)], axis=1
     )
@@ -479,25 +510,40 @@
     for s in range(shards):
         pre_grad[s, mine, node_part:] = neg_back[:, s * width : (s + 1) * width]
     piece = pre_grad.at[:, mine, pl.ds(node_part, neg_part)]
-    last = 13 * shards
-    to_x_peer.append(send(piece, piece, last, x_peer))
-    to_core_peer.append(send(piece, piece, last + 1, core_peer))
+    to_x_peer.append(send(piece, piece, x_peer))
+    to_core_peer.append(send(piece, piece, core_peer))
     for k in home:
         to_x_peer[k].wait_recv()
         piece = pre_grad.at[sources[k], crossed, pl.ds(0, node_part)]
-        passed.append(send(piece, piece, 12 * shards + k, core_peer))
+        passed.append(send(piece, piece, core_peer))
     to_x_peer[shards].wait_recv()
     piece = pre_grad.at[:, crossed, pl.ds(node_part, neg_part)]
-    passed.append(send(piece, piece, last + 2, core_peer))
+    passed.append(send(piece, piece, core_peer))
     placed = (
         lax.broadcasted_iota(jnp.int32, (node_count, neg_count), 0) == neg_line[...]
     ).astype(bf16)
     for copy in to_core_peer + passed:
         copy.wait_recv()
-    for s in range(shards):
-        node_grad = pre_grad[s, :, :node_part].reshape(node_count, width).astype(f32)
-        neg_grad = pre_grad[s, :, node_part:].reshape(neg_count, width)
-        out[:, s * width : (s + 1) * width] = (node_grad + dot(placed, neg_grad)).astype(bf16)
+    node_grad = jnp.concatenate(
+        [pre_grad[s, :, :node_part].reshape(node_count, width) for s in range(shards)], axis=1
+    )
+    neg_grad = jnp.concatenate(
+        [pre_grad[s, :, node_part:].reshape(neg_count, width) for s in range(shards)], axis=1
+    )
+    summed[...] = (node_grad.astype(f32) + dot(placed, neg_grad)).astype(bf16)
+    feat_tile = out.shape[1] // 4
+
+    def out_tile(f, carry):
+        columns = pl.ds(pl.multiple_of(f * feat_tile, feat_tile), feat_tile)
+        total = dot(summed[:, 0:tile], projection[0, columns], 1, 1)
+        for t in range(1, tiles):
+            total = total + dot(
+                summed[:, t * tile : (t + 1) * tile], projection[t, columns], 1, 1
+            )
+        out[:, columns] = total
+        return carry
+
+    lax.fori_loop(0, 4, out_tile, 0)
     for copy in sent:
         copy.wait_send()
 
@@ -514,13 +560,13 @@
     f32, bf16 = jnp.float32, jnp.bfloat16
     owner_line = jnp.transpose(slot_owner, (1, 2, 0)).reshape(slot_count, query_count)
     sizes = (shards, slot_count, node_count, neg_count, query_count)
-    sems = 13 * shards + 3
+    sems = 18 * shards
     tiles = embed_width // (2 * width)
     hbm = pl.BlockSpec(memory_space=pl.ANY)
     vmem = pl.BlockSpec(memory_space=pltpu.VMEM)
-    pre_grad = pl.pallas_call(
+    return pl.pallas_call(
         functools.partial(kernel, sizes),
-        out_shape=jax.ShapeDtypeStruct((node_count, embed_width), bf16),
+        out_shape=jax.ShapeDtypeStruct((node_count, feat_width), f32),
         in_specs=[hbm] * 2 + [vmem] * 4,
         out_specs=vmem,
         scratch_shapes=[
@@ -530,6 +576,7 @@
             pltpu.VMEM((query_count, width), f32),
             pltpu.VMEM((part, embed_width), f32),
             pltpu.VMEM((shards, width, node_count), f32),
+            pltpu.VMEM((node_count, embed_width), bf16),
             pltpu.VMEM((4 * part, feat_width), bf16),
             pltpu.VMEM((4, part, embed_width), f32),
             pltpu.VMEM((4, part, embed_width), f32),
@@ -567,7 +614,6 @@
         jnp.transpose(visits),
         neg_row.reshape(1, neg_count),
     )
-    return times_back(pre_grad, projection)
 
 
 def solution(mesh):

time: 68.6 us -> 67.3 us (0.981)
  matrix products: 2.76 us -> 0 us
  local copies, waits for them, and re-layouts: 0.01 us -> 2.31 us
  Pallas kernels: 65.6 us -> 64.8 us
    dot_general x1 -> x0, matrix products: 2.76 us -> none  [times_back(): jnp.einsum('re,fe->rf', left, projection, preferred_element_type=jnp.floa...]
    unnamed x2 -> x1, local copies, waits for them, and re-layouts: 0.01 us -> 2.31 us
    pallas_call x1, Pallas kernels: 65.6 us -> 64.8 us  [column_split(): pl.pallas_call(functools.partial(kernel, sizes), out_shape=jax.ShapeDtype...]
where the time goes in v4:
time: 67.3 us; the launch traced here: 67.1 us
  Pallas kernels  64.8 us (96%)
  local copies, waits for them, and re-layouts  2.31 us (3%)
    pallas_call x1, Pallas kernels, column_split(): pl.pallas_call(functools.partial(kernel, sizes), out_shape=jax.ShapeDtype...  64.8 us
    unnamed x1, local copies, waits for them, and re-layouts  2.31 us

profile of v4, /device:TPU:1, one launch (start us, length us, event | category | flops | bytes accessed | tf_op | source)
XLA Modules:
  0.0 67.1 jit_solution(907035009869392632)
XLA Ops:
  0.0 64.8 %shard_map.64 = f32[256,1024]{1,0:T(8,128)} custom-call(bf16[256,1024]{1,0:T(8,128)(2,1)} %table_hbm.1, bf16[1024,1024]{1,0:T(8,128)(2,1)} %projection_hbm.1, s32[16,32]{1,0:T(8,128)} %bitcast.8, s32[16,32]{1,0:T(8,128)} %bitcast.9, s32[13,32]{1,0:T(8,128)} %bitcast.10, s32[1,64]{1,0:T(1,128)} %bitcast.11), custom_call_target="tpu_custom_call" | custom-call | tf_op jit(solution)/shard_map/pallas_call | solution.py:567
  64.8 2.3 %copy.9 = f32[256,1024]{1,0:T(8,128)} copy(f32[256,1024]{1,0:T(8,128)} %shard_map.64) | data formatting | bytes 2097152

commit v5 on v4

--- a/solution.py
+++ b/solution.py
@@ -262,14 +262,13 @@
         pl.semaphore_signal(barrier, inc=1, device_id=device, device_id_type=MESH)
 
     lines[...] = jnp.zeros(lines.shape, f32)
-    lines[0:slot_count, 0:query_count] = (
-        owner_line[...] * node_count + row_line[...]
-    ).astype(f32)
-    lines[slot_count : 2 * slot_count - 3, 0:query_count] = visit_line[...].astype(f32)
-    lines[2 * slot_count : 2 * slot_count + 1, 0:neg_count] = neg_line[...].astype(f32)
+    lines[0:slot_count, 0:query_count] = owner_line[...].astype(f32)
+    lines[slot_count : 2 * slot_count, 0:query_count] = row_line[...].astype(f32)
+    lines[2 * slot_count : 3 * slot_count - 3, 0:query_count] = visit_line[...].astype(f32)
+    lines[3 * slot_count : 3 * slot_count + 1, 0:neg_count] = neg_line[...].astype(f32)
     columns = jnp.transpose(lines[...])
     info[...] = columns[0:query_count]
-    neg_column = columns[0:neg_count, 2 * slot_count : 2 * slot_count + 1].astype(jnp.int32)
+    neg_column = columns[0:neg_count, 3 * slot_count : 3 * slot_count + 1].astype(jnp.int32)
     neg_pick = (
         lax.broadcasted_iota(jnp.int32, (neg_count, node_count), 1) == neg_column
     ).astype(bf16)
@@ -278,6 +277,14 @@
     for b in range(4):
         feats[b * part : b * part + node_part] = table[b * node_part : (b + 1) * node_part]
         feats[b * part + node_part : (b + 1) * part] = neg_feat[b * neg_part : (b + 1) * neg_part]
+    pl.semaphore_wait(barrier, shards + 1)
+
+    own_rows = pl.ds(pl.multiple_of(me * query_count, query_count), query_count)
+    info_copies = [
+        send(info, info_all.at[own_rows], (peers[k], rep)) for k in range(1, shards)
+    ]
+    info_all[own_rows] = info[...]
+    base = shards
     squares = jnp.zeros((4 * part, 1), f32)
     for t in range(tiles):
         loads[1 + t].wait()
@@ -290,14 +297,6 @@
     place = lax.broadcasted_iota(jnp.int32, (4, part, 1), 1)
     scale = jnp.where(place >= node_part, lax.rsqrt(squares + epsilon), 1.0)
 
-    pl.semaphore_wait(barrier, shards + 1)
-
-    own_rows = pl.ds(pl.multiple_of(me * query_count, query_count), query_count)
-    info_copies = [
-        send(info, info_all.at[own_rows], (peers[k], rep)) for k in range(1, shards)
-    ]
-    info_all[own_rows] = info[...]
-    base = shards
     slice_copies = []
     for k in list(range(1, shards)) + [0]:
         columns = pl.ds(pl.multiple_of(peers[k] * width, width), width)
@@ -314,21 +313,35 @@
         copy.wait_recv()
     block = 16
 
+    chunks = node_count // width
+    zero = jnp.zeros((block, width), bf16)
+    lane = lax.broadcasted_iota(jnp.int32, (block, width), 1)
+    lanes = [(lane + c * width).astype(f32).astype(bf16) for c in range(chunks)]
+
     def pick_rows(step, carry):
-        start = pl.multiple_of(step * block, block)
-        ids = info_all[pl.ds(start, block)]
-        lane = lax.broadcasted_iota(jnp.int32, (block, shards * node_count), 1).astype(f32)
-        for s in range(3):
-            picks[s, pl.ds(start, block)] = (
-                jnp.where(lane == ids[:, s : s + 1], 1.0, 0.0).astype(bf16)
-            )
-        counts = ids
-        spread = jnp.zeros(lane.shape, f32)
-        for k in range(3, slot_count):
-            spread = spread + jnp.where(
-                lane == ids[:, k : k + 1], counts[:, slot_count + k - 3 : slot_count + k - 2], 0.0
-            )
-        picks[3, pl.ds(start, block)] = spread.astype(bf16)
+        here = pl.ds(pl.multiple_of(step * block, block), block)
+        ids = info_all[here]
+
+        def wide(column):
+            return jnp.broadcast_to(ids[:, column : column + 1], (block, width)).astype(bf16)
+
+        def hits(slot, amount):
+            owner, row = wide(slot), wide(slot_count + slot)
+            found = [row == place for place in lanes]
+            for shard in range(shards):
+                held = jnp.where(owner == jnp.asarray(shard, bf16), amount, zero)
+                for c in range(chunks):
+                    yield shard * chunks + c, jnp.where(found[c], held, zero)
+
+        for slot in range(3):
+            for place, value in hits(slot, jnp.ones((block, width), bf16)):
+                picks[slot, here, place * width : (place + 1) * width] = value
+        spread = [zero] * (shards * chunks)
+        for slot in range(3, slot_count):
+            for place, value in hits(slot, wide(2 * slot_count + slot - 3)):
+                spread[place] = spread[place] + value
+        for place, value in enumerate(spread):
+            picks[3, here, place * width : (place + 1) * width] = value
         return carry
 
     over_x, over_core, twice = {}, {}, {}
@@ -370,7 +383,7 @@
             pass_twice(k + shards // 2 + 1)
         gather_from(k)
     neg_slice = slices[:, :, node_part:].reshape(shards * neg_count, width)
-    counts = info_all[:, slot_count : 2 * slot_count - 3]
+    counts = info_all[:, 2 * slot_count : 3 * slot_count - 3]
     visit_total = jnp.sum(counts, axis=1, keepdims=True)
     hood = picked[0] + picked[3] / visit_total
     pos, hard = picked[1], picked[2]
@@ -622,7 +635,8 @@
     def body(feature_table, projection, slot_owner, slot_row, visits, neg_row):
         width = projection.shape[1] // shards
         parts = (feature_table.shape[0], neg_row.shape[0], slot_row.shape[0] * 2)
-        small = slot_row.shape[0] <= 128 and neg_row.shape[0] <= 128 and slot_row.shape[1] <= 32
+        small = slot_row.shape[0] <= 128 and neg_row.shape[0] <= 128 and slot_row.shape[1] <= 40
+        small = small and feature_table.shape[0] in (width, 2 * width)
         whole = width == 128 and reps == 4 and small and all(size % 64 == 0 for size in parts)
         form = column_split if whole else on_device
         return form(feature_table, projection, slot_owner, slot_row, visits, neg_row)

time: 67.3 us -> 65 us (0.966)
  Pallas kernels: 64.8 us -> 62.5 us
    pallas_call x1, Pallas kernels: 64.8 us -> 62.5 us  [column_split(): pl.pallas_call(functools.partial(kernel, sizes), out_shape=jax.ShapeDtype...]
where the time goes in v5:
time: 65 us; the launch traced here: 64.8 us
  Pallas kernels  62.5 us (96%)
  local copies, waits for them, and re-layouts  2.31 us (4%)
    pallas_call x1, Pallas kernels, column_split(): pl.pallas_call(functools.partial(kernel, sizes), out_shape=jax.ShapeDtype...  62.5 us
    unnamed x1, local copies, waits for them, and re-layouts  2.31 us

profile of v5, /device:TPU:1, one launch (start us, length us, event | category | flops | bytes accessed | tf_op | source)
XLA Modules:
  0.0 64.8 jit_solution(12351267435302036315)
XLA Ops:
  0.0 62.5 %shard_map.64 = f32[256,1024]{1,0:T(8,128)} custom-call(bf16[256,1024]{1,0:T(8,128)(2,1)} %table_hbm.1, bf16[1024,1024]{1,0:T(8,128)(2,1)} %projection_hbm.1, s32[16,32]{1,0:T(8,128)} %bitcast.8, s32[16,32]{1,0:T(8,128)} %bitcast.9, s32[13,32]{1,0:T(8,128)} %bitcast.10, s32[1,64]{1,0:T(1,128)} %bitcast.11), custom_call_target="tpu_custom_call" | custom-call | tf_op jit(solution)/shard_map/pallas_call | solution.py:580
  62.5 2.3 %copy.9 = f32[256,1024]{1,0:T(8,128)} copy(f32[256,1024]{1,0:T(8,128)} %shard_map.64) | data formatting | bytes 2097152

commit v6 on v5

--- a/solution.py
+++ b/solution.py
@@ -185,7 +185,9 @@
     info,
     slope,
     early,
-    summed,
+    norms,
+    norms_all,
+    neg_all,
     feats,
     pre,
     act,
@@ -255,6 +257,13 @@
         sent.append(copy)
         return copy
 
+    drained = [0]
+
+    def drain(count):
+        for copy in sent[drained[0] : count]:
+            copy.wait_send()
+        drained[0] = count
+
     barrier = pltpu.get_barrier_semaphore()
     for k in range(1, shards):
         pl.semaphore_signal(barrier, inc=1, device_id=(peers[k], rep), device_id_type=MESH)
@@ -286,28 +295,31 @@
     info_all[own_rows] = info[...]
     base = shards
     squares = jnp.zeros((4 * part, 1), f32)
-    for t in range(tiles):
-        loads[1 + t].wait()
-        values = dot(feats[...], projection[t])
-        pre[:, :, t * tile : (t + 1) * tile] = values.reshape(4, part, tile)
-        values = values * jax.nn.sigmoid(values)
-        act[:, :, t * tile : (t + 1) * tile] = values.reshape(4, part, tile)
-        squares = squares + jnp.sum(values * values, axis=1, keepdims=True)
-    squares = squares.reshape(4, part, 1)
-    place = lax.broadcasted_iota(jnp.int32, (4, part, 1), 1)
-    scale = jnp.where(place >= node_part, lax.rsqrt(squares + epsilon), 1.0)
-
+    for load in loads[1:]:
+        load.wait()
     slice_copies = []
     for k in list(range(1, shards)) + [0]:
         columns = pl.ds(pl.multiple_of(peers[k] * width, width), width)
-        values = (act[:, :, columns] * scale).astype(bf16)
+        within = pl.ds(pl.multiple_of(peers[k] % 2 * width, width), width)
+        values = dot(feats[...], projection[peers[k] // 2, :, within])
+        pre[:, :, columns] = values.reshape(4, part, width)
+        values = values * jax.nn.sigmoid(values)
+        squares = squares + jnp.sum(values * values, axis=1, keepdims=True)
+        values = values.reshape(4, part, width)
+        act[:, :, columns] = values
         if k:
-            rows[k] = values
-            slice_copies.append(
-                send(rows.at[k, mine], slices.at[me, mine], (peers[k], rep))
-            )
+            rows[k] = values.astype(bf16)
+            slice_copies.append(send(rows.at[k, mine], slices.at[me, mine], (peers[k], rep)))
         else:
-            slices[me] = values
+            slices[me] = values.astype(bf16)
+    inverse = lax.rsqrt(squares.reshape(4, part, 1)[:, node_part:] + epsilon)
+    inverse = inverse.reshape(neg_count, 1)
+    if neg_count < 128:
+        inverse = jnp.concatenate([inverse, jnp.zeros((128 - neg_count, 1), f32)], axis=0)
+    inverse = jnp.transpose(jnp.broadcast_to(inverse, (128, 128)))
+    norms[...] = inverse[0:8]
+    norms_all[me] = inverse[0:8]
+    norm_copies = [send(norms, norms_all.at[me], (peers[k], rep)) for k in range(1, shards)]
 
     for copy in info_copies:
         copy.wait_recv()
@@ -382,7 +394,17 @@
         if k + shards // 2 < last:
             pass_twice(k + shards // 2 + 1)
         gather_from(k)
-    neg_slice = slices[:, :, node_part:].reshape(shards * neg_count, width)
+    for copy in norm_copies:
+        copy.wait_recv()
+    inverse = [norms_all[s, 0:1] for s in range(shards)]
+    inverse = jnp.transpose(
+        jnp.concatenate(inverse + [jnp.zeros((128 - shards, 128), f32)], axis=0)
+    )
+    for s in range(shards):
+        values = slices[s, :, node_part:].reshape(neg_count, width).astype(f32)
+        values = values * inverse[0:neg_count, s : s + 1]
+        neg_all[s * neg_count : (s + 1) * neg_count] = values.astype(bf16)
+    neg_slice = neg_all[...]
     counts = info_all[:, 2 * slot_count : 3 * slot_count - 3]
     visit_total = jnp.sum(counts, axis=1, keepdims=True)
     hood = picked[0] + picked[3] / visit_total
@@ -413,6 +435,7 @@
     neg_unit = act[mine, node_part:]
     inverse = lax.rsqrt(jnp.sum(neg_unit * neg_unit, axis=1, keepdims=True) + epsilon)
     neg_unit = neg_unit * inverse
+    drain(len(sent) - 3 * (shards - 1))
     sums = stats[own_rows]
     for copy in stat_copies:
         copy.wait_recv()
@@ -456,6 +479,7 @@
         return carry
 
     lax.fori_loop(0, shards, early_block, 0)
+    drain(len(sent) - 3 * (shards - 1))
     for copy in weight_copies:
         copy.wait_recv()
 
@@ -532,6 +556,7 @@
     to_x_peer[shards].wait_recv()
     piece = pre_grad.at[:, crossed, pl.ds(node_part, neg_part)]
     passed.append(send(piece, piece, core_peer))
+    drain(len(sent) - len(to_x_peer + to_core_peer + passed))
     placed = (
         lax.broadcasted_iota(jnp.int32, (node_count, neg_count), 0) == neg_line[...]
     ).astype(bf16)
@@ -543,22 +568,8 @@
     neg_grad = jnp.concatenate(
         [pre_grad[s, :, node_part:].reshape(neg_count, width) for s in range(shards)], axis=1
     )
-    summed[...] = (node_grad.astype(f32) + dot(placed, neg_grad)).astype(bf16)
-    feat_tile = out.shape[1] // 4
-
-    def out_tile(f, carry):
-        columns = pl.ds(pl.multiple_of(f * feat_tile, feat_tile), feat_tile)
-        total = dot(summed[:, 0:tile], projection[0, columns], 1, 1)
-        for t in range(1, tiles):
-            total = total + dot(
-                summed[:, t * tile : (t + 1) * tile], projection[t, columns], 1, 1
-            )
-        out[:, columns] = total
-        return carry
-
-    lax.fori_loop(0, 4, out_tile, 0)
-    for copy in sent:
-        copy.wait_send()
+    out[...] = (node_grad.astype(f32) + dot(placed, neg_grad)).astype(bf16)
+    drain(len(sent))
 
 
 def column_split(feature_table, projection, slot_owner, slot_row, visits, neg_row):
@@ -573,13 +584,13 @@
     f32, bf16 = jnp.float32, jnp.bfloat16
     owner_line = jnp.transpose(slot_owner, (1, 2, 0)).reshape(slot_count, query_count)
     sizes = (shards, slot_count, node_count, neg_count, query_count)
-    sems = 18 * shards
+    sems = 19 * shards
     tiles = embed_width // (2 * width)
     hbm = pl.BlockSpec(memory_space=pl.ANY)
     vmem = pl.BlockSpec(memory_space=pltpu.VMEM)
-    return pl.pallas_call(
+    pre_grad = pl.pallas_call(
         functools.partial(kernel, sizes),
-        out_shape=jax.ShapeDtypeStruct((node_count, feat_width), f32),
+        out_shape=jax.ShapeDtypeStruct((node_count, embed_width), bf16),
         in_specs=[hbm] * 2 + [vmem] * 4,
         out_specs=vmem,
         scratch_shapes=[
@@ -589,7 +600,9 @@
             pltpu.VMEM((query_count, width), f32),
             pltpu.VMEM((part, embed_width), f32),
             pltpu.VMEM((shards, width, node_count), f32),
-            pltpu.VMEM((node_count, embed_width), bf16),
+            pltpu.VMEM((8, 128), f32),
+            pltpu.VMEM((shards, 8, 128), f32),
+            pltpu.VMEM((shards * neg_count, width), bf16),
             pltpu.VMEM((4 * part, feat_width), bf16),
             pltpu.VMEM((4, part, embed_width), f32),
             pltpu.VMEM((4, part, embed_width), f32),
@@ -617,7 +630,7 @@
             pltpu.SemaphoreType.DMA((tiles + 1,)),
         ],
         compiler_params=pltpu.CompilerParams(
-            collective_id=0, has_side_effects=True, vmem_limit_bytes=60 * 1024 * 1024
+            collective_id=0, has_side_effects=True, vmem_limit_bytes=56 * 1024 * 1024
         ),
     )(
         feature_table,
@@ -627,6 +640,7 @@
         jnp.transpose(visits),
         neg_row.reshape(1, neg_count),
     )
+    return times_back(pre_grad, projection)
 
 
 def solution(mesh):
@@ -636,7 +650,7 @@
         width = projection.shape[1] // shards
         parts = (feature_table.shape[0], neg_row.shape[0], slot_row.shape[0] * 2)
         small = slot_row.shape[0] <= 128 and neg_row.shape[0] <= 128 and slot_row.shape[1] <= 40
-        small = small and feature_table.shape[0] in (width, 2 * width)
+        small = small and shards <= 128 and feature_table.shape[0] in (width, 2 * width)
         whole = width == 128 and reps == 4 and small and all(size % 64 == 0 for size in parts)
         form = column_split if whole else on_device
         return form(feature_table, projection, slot_owner, slot_row, visits, neg_row)

time: 65 us -> 65.1 us (level)
  matrix products: 0 us -> 2.76 us
  local copies, waits for them, and re-layouts: 2.31 us -> 0.01 us
    dot_general x0 -> x1, matrix products: none -> 2.76 us  [times_back(): jnp.einsum('re,fe->rf', left, projection, preferred_element_type=jnp.floa...]
    unnamed x1 -> x2, local copies, waits for them, and re-layouts: 2.31 us -> 0.01 us
where the time goes in v6:
time: 65.1 us; the launch traced here: 64.9 us
  Pallas kernels  62.1 us (95%)
  matrix products  2.76 us (4%)
    pallas_call x1, Pallas kernels, column_split(): pl.pallas_call(functools.partial(kernel, sizes), out_shape=jax.ShapeDtype...  62.1 us
    dot_general x1, matrix products, times_back(): jnp.einsum('re,fe->rf', left, projection, preferred_element_type=jnp.floa...  2.76 us

profile of v6, /device:TPU:1, one launch (start us, length us, event | category | flops | bytes accessed | tf_op | source)
XLA Modules:
  0.0 64.9 jit_solution(6307793325803835497)
XLA Ops:
  0.0 0.0 copy-start
  0.0 62.1 %shard_map.64 = bf16[256,1024]{1,0:T(8,128)(2,1)} custom-call(bf16[256,1024]{1,0:T(8,128)(2,1)} %table_hbm.1, bf16[1024,1024]{1,0:T(8,128)(2,1)} %projection_hbm.1, s32[16,32]{1,0:T(8,128)} %bitcast.10, s32[16,32]{1,0:T(8,128)} %bitcast.11, s32[13,32]{1,0:T(8,128)} %bitcast.12, s32[1,64]{1,0:T(1,128)} %bitcast.13), custom_call_target="tpu_custom_call" | custom-call | tf_op jit(solution)/shard_map/pallas_call | solution.py:591
  62.1 0.0 copy-done
  62.1 2.8 %fusion = f32[256,1024]{1,0:T(8,128)} fusion(bf16[256,1024]{1,0:T(8,128)(2,1)} %shard_map.64, bf16[1024,1024]{1,0:T(8,128)(2,1)S(1)} %copy-done), kind=kOutput, calls=%fused_computation | convolution fusion | flops 536870912 | bytes 3670016 | tf_op jit(solution)/shard_map/re,fe->rf/dot_general | solution.py:32
Async XLA Ops:
  0.0 62.1 %copy-start = (bf16[1024,1024]{1,0:T(8,128)(2,1)S(1)}, bf16[1024,1024]{1,0:T(8,128)(2,1)}, u32[]{:S(2)}) copy-start(bf16[1024,1024]{1,0:T(8,128)(2,1)} %projection_hbm.1) | copy-start | bytes 6291460

commit v7 on v6

--- a/solution.py
+++ b/solution.py
@@ -187,6 +187,8 @@
     early,
     norms,
     norms_all,
+    own_scalars,
+    scalars_in,
     neg_all,
     feats,
     pre,
@@ -276,7 +278,7 @@
     lines[2 * slot_count : 3 * slot_count - 3, 0:query_count] = visit_line[...].astype(f32)
     lines[3 * slot_count : 3 * slot_count + 1, 0:neg_count] = neg_line[...].astype(f32)
     columns = jnp.transpose(lines[...])
-    info[...] = columns[0:query_count]
+    info[...] = columns[0:query_count].astype(bf16)
     neg_column = columns[0:neg_count, 3 * slot_count : 3 * slot_count + 1].astype(jnp.int32)
     neg_pick = (
         lax.broadcasted_iota(jnp.int32, (neg_count, node_count), 1) == neg_column
@@ -332,7 +334,7 @@
 
     def pick_rows(step, carry):
         here = pl.ds(pl.multiple_of(step * block, block), block)
-        ids = info_all[here]
+        ids = info_all[here].astype(f32)
 
         def wide(column):
             return jnp.broadcast_to(ids[:, column : column + 1], (block, width)).astype(bf16)
@@ -405,7 +407,7 @@
         values = values * inverse[0:neg_count, s : s + 1]
         neg_all[s * neg_count : (s + 1) * neg_count] = values.astype(bf16)
     neg_slice = neg_all[...]
-    counts = info_all[:, 2 * slot_count : 3 * slot_count - 3]
+    counts = info_all[...].astype(f32)[:, 2 * slot_count : 3 * slot_count - 3]
     visit_total = jnp.sum(counts, axis=1, keepdims=True)
     hood = picked[0] + picked[3] / visit_total
     pos, hard = picked[1], picked[2]
@@ -425,23 +427,30 @@
         ]
 
     score_copies = [send_half(0)]
-    stats[...] = lanes_of([jnp.sum(a * b, axis=1, keepdims=True) for a, b in pairs], width)
+    flat = jnp.transpose(
+        lanes_of([jnp.sum(a * b, axis=1, keepdims=True) for a, b in pairs], width)
+    )
+    rest = jnp.zeros((8, 128 - query_count), f32)
+    for s in range(shards):
+        stats[s] = jnp.concatenate(
+            [flat[0:8, s * query_count : (s + 1) * query_count], rest], axis=1
+        )
     stat_copies = []
     for k in range(1, shards):
-        there = pl.ds(pl.multiple_of(peers[k] * query_count, query_count), query_count)
-        stat_copies.append(send(stats.at[there], stats_all.at[k], (peers[k], rep)))
+        stat_copies.append(send(stats.at[peers[k]], stats_all.at[k], (peers[k], rep)))
     score_copies.append(send_half(1))
     slope[...] = silu_slope(pre[mine])
     neg_unit = act[mine, node_part:]
     inverse = lax.rsqrt(jnp.sum(neg_unit * neg_unit, axis=1, keepdims=True) + epsilon)
     neg_unit = neg_unit * inverse
     drain(len(sent) - 3 * (shards - 1))
-    sums = stats[own_rows]
+    sums = stats[me]
     for copy in stat_copies:
         copy.wait_recv()
     for k in range(1, shards):
         sums = sums + stats_all[k]
-    weight_copies, copies = [], []
+    sums = jnp.transpose(jnp.concatenate([sums, jnp.zeros((120, 128), f32)], axis=0))
+    weight_copies, copies, halves = [], [], []
     for h in range(2):
         there = half_rows(me, h)
         dots = partial[there].astype(f32)
@@ -452,11 +461,14 @@
             dots = dots + parts[k, held].astype(f32)
         weight, scalars = loss_weights(dots, sums[held])
         weight_all[there] = weight
-        scalar_all[there] = lanes_of(scalars, width)
+        halves.append(lanes_of(scalars, 128))
         if h:
+            rest = jnp.zeros((128 - query_count, 128), f32)
+            flat = jnp.transpose(jnp.concatenate(halves + [rest], axis=0))
+            own_scalars[...] = flat[0:8]
+            scalars_in[me] = flat[0:8]
             copies = [
-                send(scalar_all.at[own_rows], scalar_all.at[own_rows], (peers[k], rep))
-                for k in range(1, shards)
+                send(own_scalars, scalars_in.at[me], (peers[k], rep)) for k in range(1, shards)
             ]
         for k in range(1, shards):
             weight_copies.append(
@@ -464,7 +476,15 @@
             )
     for copy in copies:
         copy.wait_recv()
-    scalars = scalar_all[...]
+    flat = [scalars_in[s] for s in range(shards)]
+    if shards < 16:
+        flat.append(jnp.zeros((128 - 8 * shards, 128), f32))
+    flat = jnp.transpose(jnp.concatenate(flat, axis=0))
+    for s in range(shards):
+        scalar_all[s * query_count : (s + 1) * query_count, 0:8] = flat[
+            0:query_count, s * 8 : (s + 1) * 8
+        ]
+    scalars = scalar_all[:, 0:8]
     side = item_side(hood, pos, hard, scalars)
     query_unit, query_float, known_grad, pos_grad, hard_grad = side
     flipped[:, 0:group] = jnp.transpose(pos_grad).astype(bf16)
@@ -597,24 +617,26 @@
             pltpu.VMEM((node_count, feat_width), bf16),
             pltpu.VMEM((tiles, feat_width, 2 * width), bf16),
             pltpu.VMEM((128, 128), f32),
-            pltpu.VMEM((query_count, width), f32),
+            pltpu.VMEM((query_count, width), bf16),
             pltpu.VMEM((part, embed_width), f32),
             pltpu.VMEM((shards, width, node_count), f32),
+            pltpu.VMEM((8, 128), f32),
+            pltpu.VMEM((shards, 8, 128), f32),
             pltpu.VMEM((8, 128), f32),
             pltpu.VMEM((shards, 8, 128), f32),
             pltpu.VMEM((shards * neg_count, width), bf16),
             pltpu.VMEM((4 * part, feat_width), bf16),
             pltpu.VMEM((4, part, embed_width), f32),
             pltpu.VMEM((4, part, embed_width), f32),
-            pltpu.VMEM((group, width), f32),
+            pltpu.VMEM((group, width), bf16),
             pltpu.VMEM((shards, 4, part, width), bf16),
             pltpu.VMEM((shards, 4, part, width), bf16),
             pltpu.VMEM((4, group, shards * node_count), bf16),
             pltpu.VMEM((4, group, width), f32),
             pltpu.VMEM((group, shards * neg_count), bf16),
             pltpu.VMEM((shards, query_count, shards * neg_count), bf16),
-            pltpu.VMEM((group, width), f32),
-            pltpu.VMEM((shards, query_count, width), f32),
+            pltpu.VMEM((shards, 8, 128), f32),
+            pltpu.VMEM((shards, 8, 128), f32),
             pltpu.VMEM((group, shards * neg_count), bf16),
             pltpu.VMEM((group, width), f32),
             pltpu.VMEM((width, 4 * group), bf16),
@@ -649,8 +671,8 @@
     def body(feature_table, projection, slot_owner, slot_row, visits, neg_row):
         width = projection.shape[1] // shards
         parts = (feature_table.shape[0], neg_row.shape[0], slot_row.shape[0] * 2)
-        small = slot_row.shape[0] <= 128 and neg_row.shape[0] <= 128 and slot_row.shape[1] <= 40
-        small = small and shards <= 128 and feature_table.shape[0] in (width, 2 * width)
+        small = slot_row.shape[0] < 128 and neg_row.shape[0] <= 128 and slot_row.shape[1] <= 40
+        small = small and shards <= 16 and feature_table.shape[0] in (width, 2 * width)
         whole = width == 128 and reps == 4 and small and all(size % 64 == 0 for size in parts)
         form = column_split if whole else on_device
         return form(feature_table, projection, slot_owner, slot_row, visits, neg_row)

time: 65.1 us -> 58.6 us (0.900)
  Pallas kernels: 62.1 us -> 55.7 us
    pallas_call x1, Pallas kernels: 62.1 us -> 55.7 us  [column_split(): pl.pallas_call(functools.partial(kernel, sizes), out_shape=jax.ShapeDtype...]
where the time goes in v7:
time: 58.6 us; the launch traced here: 58.5 us
  Pallas kernels  55.7 us (95%)
  matrix products  2.76 us (5%)
    pallas_call x1, Pallas kernels, column_split(): pl.pallas_call(functools.partial(kernel, sizes), out_shape=jax.ShapeDtype...  55.7 us
    dot_general x1, matrix products, times_back(): jnp.einsum('re,fe->rf', left, projection, preferred_element_type=jnp.floa...  2.76 us

profile of v7, /device:TPU:1, one launch (start us, length us, event | category | flops | bytes accessed | tf_op | source)
XLA Modules:
  0.0 58.5 jit_solution(14228241506587187063)
XLA Ops:
  0.0 0.0 copy-start
  0.0 55.7 %shard_map.64 = bf16[256,1024]{1,0:T(8,128)(2,1)} custom-call(bf16[256,1024]{1,0:T(8,128)(2,1)} %table_hbm.1, bf16[1024,1024]{1,0:T(8,128)(2,1)} %projection_hbm.1, s32[16,32]{1,0:T(8,128)} %bitcast.10, s32[16,32]{1,0:T(8,128)} %bitcast.11, s32[13,32]{1,0:T(8,128)} %bitcast.12, s32[1,64]{1,0:T(1,128)} %bitcast.13), custom_call_target="tpu_custom_call" | custom-call | tf_op jit(solution)/shard_map/pallas_call | solution.py:611
  55.7 0.0 copy-done
  55.7 2.8 %fusion = f32[256,1024]{1,0:T(8,128)} fusion(bf16[256,1024]{1,0:T(8,128)(2,1)} %shard_map.64, bf16[1024,1024]{1,0:T(8,128)(2,1)S(1)} %copy-done), kind=kOutput, calls=%fused_computation | convolution fusion | flops 536870912 | bytes 3670016 | tf_op jit(solution)/shard_map/re,fe->rf/dot_general | solution.py:32
Async XLA Ops:
  0.0 55.7 %copy-start = (bf16[1024,1024]{1,0:T(8,128)(2,1)S(1)}, bf16[1024,1024]{1,0:T(8,128)(2,1)}, u32[]{:S(2)}) copy-start(bf16[1024,1024]{1,0:T(8,128)(2,1)} %projection_hbm.1) | copy-start | bytes 6291460

commit v8 on v7

--- a/solution.py
+++ b/solution.py
@@ -139,6 +139,25 @@
     return result
 
 
+def pack_lines(tile, start, count):
+    each = 128 // count
+    lines = []
+    for i in range(0, 8, each):
+        pieces = [tile[i + j : i + j + 1, start : start + count] for j in range(each)]
+        lines.append(jnp.concatenate(pieces, axis=1))
+    return jnp.concatenate(lines, axis=0)
+
+
+def unpack_lines(packed, count):
+    each = 128 // count
+    pieces = [
+        packed[i // each : i // each + 1, i % each * count : (i % each + 1) * count]
+        for i in range(8)
+    ]
+    lines = jnp.concatenate(pieces, axis=0)
+    return jnp.concatenate([lines, jnp.zeros((8, 128 - count), jnp.float32)], axis=1)
+
+
 def loss_weights(dots, stats):
     inverse = lax.rsqrt(stats[:, 0:3] + epsilon)
     inv_q, inv_p, inv_h = inverse[:, 0:1], inverse[:, 1:2], inverse[:, 2:3]
@@ -183,6 +202,7 @@
     projection,
     lines,
     info,
+    info_in,
     slope,
     early,
     norms,
@@ -272,14 +292,17 @@
     for device in (x_peer, core_peer):
         pl.semaphore_signal(barrier, inc=1, device_id=device, device_id_type=MESH)
 
+    gap = jnp.zeros((3, query_count), f32)
+    pieces = [
+        owner_line[...].astype(f32),
+        row_line[...].astype(f32),
+        jnp.concatenate([visit_line[...].astype(f32), gap], axis=0),
+        jnp.zeros((slot_count, 128 - 3 * query_count), f32),
+    ]
+    info[...] = jnp.concatenate(pieces, axis=1).astype(bf16)
     lines[...] = jnp.zeros(lines.shape, f32)
-    lines[0:slot_count, 0:query_count] = owner_line[...].astype(f32)
-    lines[slot_count : 2 * slot_count, 0:query_count] = row_line[...].astype(f32)
-    lines[2 * slot_count : 3 * slot_count - 3, 0:query_count] = visit_line[...].astype(f32)
-    lines[3 * slot_count : 3 * slot_count + 1, 0:neg_count] = neg_line[...].astype(f32)
-    columns = jnp.transpose(lines[...])
-    info[...] = columns[0:query_count].astype(bf16)
-    neg_column = columns[0:neg_count, 3 * slot_count : 3 * slot_count + 1].astype(jnp.int32)
+    lines[0:1, 0:neg_count] = neg_line[...].astype(f32)
+    neg_column = jnp.transpose(lines[...])[0:neg_count, 0:1].astype(jnp.int32)
     neg_pick = (
         lax.broadcasted_iota(jnp.int32, (neg_count, node_count), 1) == neg_column
     ).astype(bf16)
@@ -292,9 +315,9 @@
 
     own_rows = pl.ds(pl.multiple_of(me * query_count, query_count), query_count)
     info_copies = [
-        send(info, info_all.at[own_rows], (peers[k], rep)) for k in range(1, shards)
+        send(info, info_in.at[me], (peers[k], rep)) for k in range(1, shards)
     ]
-    info_all[own_rows] = info[...]
+    info_in[me] = info[...]
     base = shards
     squares = jnp.zeros((4 * part, 1), f32)
     for load in loads[1:]:
@@ -319,12 +342,23 @@
     if neg_count < 128:
         inverse = jnp.concatenate([inverse, jnp.zeros((128 - neg_count, 1), f32)], axis=0)
     inverse = jnp.transpose(jnp.broadcast_to(inverse, (128, 128)))
-    norms[...] = inverse[0:8]
-    norms_all[me] = inverse[0:8]
+    norms[...] = inverse[0:1]
+    norms_all[me] = inverse[0:1]
     norm_copies = [send(norms, norms_all.at[me], (peers[k], rep)) for k in range(1, shards)]
 
     for copy in info_copies:
         copy.wait_recv()
+    turn = [info_in[s].astype(f32) for s in range(shards)]
+    if shards * slot_count < 128:
+        turn.append(jnp.zeros((128 - shards * slot_count, 128), f32))
+    turn = jnp.transpose(jnp.concatenate(turn, axis=0))
+    for s in range(shards):
+        pieces = [
+            turn[j * query_count : (j + 1) * query_count, s * slot_count : (s + 1) * slot_count]
+            for j in range(3)
+        ]
+        pieces.append(jnp.zeros((query_count, width - 3 * slot_count), f32))
+        info_all[s * query_count : (s + 1) * query_count] = jnp.concatenate(pieces, axis=1)
     block = 16
 
     chunks = node_count // width
@@ -334,7 +368,7 @@
 
     def pick_rows(step, carry):
         here = pl.ds(pl.multiple_of(step * block, block), block)
-        ids = info_all[here].astype(f32)
+        ids = info_all[here]
 
         def wide(column):
             return jnp.broadcast_to(ids[:, column : column + 1], (block, width)).astype(bf16)
@@ -398,7 +432,7 @@
         gather_from(k)
     for copy in norm_copies:
         copy.wait_recv()
-    inverse = [norms_all[s, 0:1] for s in range(shards)]
+    inverse = [norms_all[s] for s in range(shards)]
     inverse = jnp.transpose(
         jnp.concatenate(inverse + [jnp.zeros((128 - shards, 128), f32)], axis=0)
     )
@@ -407,7 +441,7 @@
         values = values * inverse[0:neg_count, s : s + 1]
         neg_all[s * neg_count : (s + 1) * neg_count] = values.astype(bf16)
     neg_slice = neg_all[...]
-    counts = info_all[...].astype(f32)[:, 2 * slot_count : 3 * slot_count - 3]
+    counts = info_all[:, 2 * slot_count : 3 * slot_count - 3]
     visit_total = jnp.sum(counts, axis=1, keepdims=True)
     hood = picked[0] + picked[3] / visit_total
     pos, hard = picked[1], picked[2]
@@ -430,11 +464,8 @@
     flat = jnp.transpose(
         lanes_of([jnp.sum(a * b, axis=1, keepdims=True) for a, b in pairs], width)
     )
-    rest = jnp.zeros((8, 128 - query_count), f32)
     for s in range(shards):
-        stats[s] = jnp.concatenate(
-            [flat[0:8, s * query_count : (s + 1) * query_count], rest], axis=1
-        )
+        stats[s] = pack_lines(flat, s * query_count, query_count)
     stat_copies = []
     for k in range(1, shards):
         stat_copies.append(send(stats.at[peers[k]], stats_all.at[k], (peers[k], rep)))
@@ -449,6 +480,7 @@
         copy.wait_recv()
     for k in range(1, shards):
         sums = sums + stats_all[k]
+    sums = unpack_lines(sums, query_count)
     sums = jnp.transpose(jnp.concatenate([sums, jnp.zeros((120, 128), f32)], axis=0))
     weight_copies, copies, halves = [], [], []
     for h in range(2):
@@ -465,8 +497,8 @@
         if h:
             rest = jnp.zeros((128 - query_count, 128), f32)
             flat = jnp.transpose(jnp.concatenate(halves + [rest], axis=0))
-            own_scalars[...] = flat[0:8]
-            scalars_in[me] = flat[0:8]
+            own_scalars[...] = pack_lines(flat, 0, query_count)
+            scalars_in[me] = pack_lines(flat, 0, query_count)
             copies = [
                 send(own_scalars, scalars_in.at[me], (peers[k], rep)) for k in range(1, shards)
             ]
@@ -476,7 +508,7 @@
             )
     for copy in copies:
         copy.wait_recv()
-    flat = [scalars_in[s] for s in range(shards)]
+    flat = [unpack_lines(scalars_in[s], query_count) for s in range(shards)]
     if shards < 16:
         flat.append(jnp.zeros((128 - 8 * shards, 128), f32))
     flat = jnp.transpose(jnp.concatenate(flat, axis=0))
@@ -617,26 +649,27 @@
             pltpu.VMEM((node_count, feat_width), bf16),
             pltpu.VMEM((tiles, feat_width, 2 * width), bf16),
             pltpu.VMEM((128, 128), f32),
-            pltpu.VMEM((query_count, width), bf16),
+            pltpu.VMEM((slot_count, 128), bf16),
+            pltpu.VMEM((shards, slot_count, 128), bf16),
             pltpu.VMEM((part, embed_width), f32),
             pltpu.VMEM((shards, width, node_count), f32),
-            pltpu.VMEM((8, 128), f32),
-            pltpu.VMEM((shards, 8, 128), f32),
-            pltpu.VMEM((8, 128), f32),
-            pltpu.VMEM((shards, 8, 128), f32),
+            pltpu.VMEM((1, 128), f32),
+            pltpu.VMEM((shards, 1, 128), f32),
+            pltpu.VMEM((8 * query_count // 128, 128), f32),
+            pltpu.VMEM((shards, 8 * query_count // 128, 128), f32),
             pltpu.VMEM((shards * neg_count, width), bf16),
             pltpu.VMEM((4 * part, feat_width), bf16),
             pltpu.VMEM((4, part, embed_width), f32),
             pltpu.VMEM((4, part, embed_width), f32),
-            pltpu.VMEM((group, width), bf16),
+            pltpu.VMEM((group, width), f32),
             pltpu.VMEM((shards, 4, part, width), bf16),
             pltpu.VMEM((shards, 4, part, width), bf16),
             pltpu.VMEM((4, group, shards * node_count), bf16),
             pltpu.VMEM((4, group, width), f32),
             pltpu.VMEM((group, shards * neg_count), bf16),
             pltpu.VMEM((shards, query_count, shards * neg_count), bf16),
-            pltpu.VMEM((shards, 8, 128), f32),
-            pltpu.VMEM((shards, 8, 128), f32),
+            pltpu.VMEM((shards, 8 * query_count // 128, 128), f32),
+            pltpu.VMEM((shards, 8 * query_count // 128, 128), f32),
             pltpu.VMEM((group, shards * neg_count), bf16),
             pltpu.VMEM((group, width), f32),
             pltpu.VMEM((width, 4 * group), bf16),
@@ -671,8 +704,8 @@
     def body(feature_table, projection, slot_owner, slot_row, visits, neg_row):
         width = projection.shape[1] // shards
         parts = (feature_table.shape[0], neg_row.shape[0], slot_row.shape[0] * 2)
-        small = slot_row.shape[0] < 128 and neg_row.shape[0] <= 128 and slot_row.shape[1] <= 40
-        small = small and shards <= 16 and feature_table.shape[0] in (width, 2 * width)
+        small = slot_row.shape[0] < 128 and neg_row.shape[0] <= 128 and slot_row.shape[1] == 16
+        small = small and shards <= 8 and 4 * slot_row.shape[0] == 128 and feature_table.shape[0] in (width, 2 * width)
         whole = width == 128 and reps == 4 and small and all(size % 64 == 0 for size in parts)
         form = column_split if whole else on_device
         return form(feature_table, projection, slot_owner, slot_row, visits, neg_row)

time: 58.6 us -> 58.3 us (level)
  Pallas kernels: 55.7 us -> 55.1 us
    pallas_call x1, Pallas kernels: 55.7 us -> 55.1 us  [column_split(): pl.pallas_call(functools.partial(kernel, sizes), out_shape=jax.ShapeDtype...]
where the time goes in v8:
time: 58.3 us; the launch traced here: 57.9 us
  Pallas kernels  55.1 us (95%)
  matrix products  2.76 us (5%)
    pallas_call x1, Pallas kernels, column_split(): pl.pallas_call(functools.partial(kernel, sizes), out_shape=jax.ShapeDtype...  55.1 us
    dot_general x1, matrix products, times_back(): jnp.einsum('re,fe->rf', left, projection, preferred_element_type=jnp.floa...  2.76 us

profile of v8, /device:TPU:1, one launch (start us, length us, event | category | flops | bytes accessed | tf_op | source)
XLA Modules:
  0.0 57.9 jit_solution(6678578476099298596)
XLA Ops:
  0.0 0.0 copy-start
  0.0 55.1 %shard_map.64 = bf16[256,1024]{1,0:T(8,128)(2,1)} custom-call(bf16[256,1024]{1,0:T(8,128)(2,1)} %table_hbm.1, bf16[1024,1024]{1,0:T(8,128)(2,1)} %projection_hbm.1, s32[16,32]{1,0:T(8,128)} %bitcast.10, s32[16,32]{1,0:T(8,128)} %bitcast.11, s32[13,32]{1,0:T(8,128)} %bitcast.12, s32[1,64]{1,0:T(1,128)} %bitcast.13), custom_call_target="tpu_custom_call" | custom-call | tf_op jit(solution)/shard_map/pallas_call | solution.py:643
  55.1 0.0 copy-done
  55.1 2.8 %fusion = f32[256,1024]{1,0:T(8,128)} fusion(bf16[256,1024]{1,0:T(8,128)(2,1)} %shard_map.64, bf16[1024,1024]{1,0:T(8,128)(2,1)S(1)} %copy-done), kind=kOutput, calls=%fused_computation | convolution fusion | flops 536870912 | bytes 3670016 | tf_op jit(solution)/shard_map/re,fe->rf/dot_general | solution.py:32
Async XLA Ops:
  0.0 55.1 %copy-start = (bf16[1024,1024]{1,0:T(8,128)(2,1)S(1)}, bf16[1024,1024]{1,0:T(8,128)(2,1)}, u32[]{:S(2)}) copy-start(bf16[1024,1024]{1,0:T(8,128)(2,1)} %projection_hbm.1) | copy-start | bytes 6291460
